TPU v7x, 32 devices: a whole 2x2x4 slice. The times are simulated.
32 devices in a mesh: row: 8 (over z, x), col: 4 (over y, core).
Axes of the slice: x: 2, y: 2, z: 4, core: 2. Of those that a mesh axis runs over, the one named last changes fastest.
Arguments:
- stereo_neuron_outputs: bfloat16 [2, 64, 64, 512], P(None, 'row', None, 'col'), may hold values from -6 to 6
- filter_tap_coefficients: bfloat16 [3, 3, 3, 64, 64], replicated, may hold values from -0.25 to 0.25
- filter_stack_intercepts: float32 [3, 64], replicated, may hold values from -3 to 3
- reference_picture_present: int32 [64, 512], P('row', 'col'), may hold values 0 or 1
- tile_shift_amounts: int32 [8, 4], P('row', 'col'), may hold values from 0 to 256, as said below
- smoothness_charges: int32 [2], replicated, may hold values from 4 to 96, as said below
Outputs:
- aggregated: float32 [64, 512, 128], P('row', 'col')
Inputs may be any that keep to these rules, and one draw needn't show every extreme that they name: `tile_shift_amounts`: every tile's offset is a whole number of 0 to 256; some tile has exactly 256. smoothness_charges[0] lies in 4 to 16; smoothness_charges[1] is 96.
All inputs are finite; a program needn't handle non-finite values. No bound on the sum of `reference_picture_present` on one device may be relied on, other than what follows from the above.
Results may differ from a plain program's by a relative error of at most 0.006.
Values may be sent and summed in bfloat16 or wider, within the bound.
No kernel may reach another device: no remote copies, remote signals or barrier semaphores. Data moves between devices by JAX's collectives and lax.ppermute only.
A program may use at most 64 MiB of HBM per device.

v0:
```python
import jax
import jax.numpy as jnp
from jax import lax
from jax.sharding import PartitionSpec as P

DISPARITIES = 128
BLOCKS = 2


def from_behind(block, axis, distance):
    devices = range(lax.axis_size(axis))
    route = [(i - distance, i) for i in devices if i - distance in devices]
    return lax.ppermute(block, axis, route)


def extended_2(value, sides, width):
    for axis, dim in sides:
        count, length = (lax.axis_size(axis), value.shape[dim])
        up = [(i, (i + 1) % count) for i in range(count - 1)]
        down = [(j, i) for i, j in up]
        last = lax.slice_in_dim(value, length - width, length, axis=dim)
        first = lax.slice_in_dim(value, 0, width, axis=dim)
        before = lax.ppermute(last, axis, up)
        after = lax.ppermute(first, axis, down)
        value = jnp.concatenate([before, value, after], axis=dim)
    return value


def advance(state, cost_row, gentle_change_charge, steep_change_charge):
    least = jnp.min(state, axis=-1, keepdims=True)
    barrier = jnp.full(state.shape[:-1] + (1,), jnp.inf, state.dtype)
    lower = jnp.concatenate([barrier, state[..., :-1]], axis=-1)
    upper = jnp.concatenate([state[..., 1:], barrier], axis=-1)
    best = jnp.minimum(
        jnp.minimum(state, jnp.minimum(lower, upper) + gentle_change_charge),
        least + steep_change_charge,
    )
    return cost_row + best - least


def sweep(costs, incoming, gentle_change_charge, steep_change_charge, backward):

    def stepper(state, cost_row):
        fresh = advance(state, cost_row, gentle_change_charge, steep_change_charge)
        return (fresh, fresh)

    return lax.scan(stepper, incoming, costs, reverse=backward)


def block_pass(block, incoming, backward, costs, total, gentle_change_charge, steep_change_charge):
    width = incoming.shape[0]
    count = costs.shape[1] // width
    inside = jnp.logical_and(block >= 0, block < count)
    start = jnp.clip(block, 0, count - 1) * width

    def work(current):
        piece = lax.dynamic_slice_in_dim(costs, start, width, 1)
        final, layers = sweep(piece, incoming, gentle_change_charge, steep_change_charge, backward)
        before = lax.dynamic_slice_in_dim(current, start, width, 1)
        return (final, lax.dynamic_update_slice_in_dim(current, before + layers, start, 1))

    def skip(current):
        return (incoming, current)

    return lax.cond(inside, work, skip, total)


def pass_down_rows(edge, offset_by):
    return from_behind(edge.astype(jnp.bfloat16), "row", offset_by).astype(edge.dtype)


def pass_across_cols(edge, offset_by):
    return from_behind(edge, "col", offset_by)


def vertical_turn(turn, carry, costs, gentle_change_charge, steep_change_charge):
    down_sent, up_sent, total = carry
    down_in = pass_down_rows(down_sent, 1)
    up_in = pass_down_rows(up_sent, -1)
    rank = lax.axis_index("row")
    extent = lax.axis_size("row")
    down_out, total = block_pass(
        turn - rank, down_in, False, costs, total, gentle_change_charge, steep_change_charge
    )
    up_out, total = block_pass(
        turn - (extent - 1 - rank),
        up_in,
        True,
        costs,
        total,
        gentle_change_charge,
        steep_change_charge,
    )
    return (down_out, up_out, total)


def horizontal_turn(turn, carry, costs, gentle_change_charge, steep_change_charge):
    right_sent, left_outgoing_message, total = carry
    right_in = pass_across_cols(right_sent, 1)
    left_in = pass_across_cols(left_outgoing_message, -1)
    rank = lax.axis_index("col")
    extent = lax.axis_size("col")
    right_out, total = block_pass(
        turn - rank, right_in, False, costs, total, gentle_change_charge, steep_change_charge
    )
    left_out, total = block_pass(
        turn - (extent - 1 - rank),
        left_in,
        True,
        costs,
        total,
        gentle_change_charge,
        steep_change_charge,
    )
    return (right_out, left_out, total)


def conv_stack(stereo_neuron_outputs, filter_tap_coefficients, filter_stack_intercepts):
    layers_total = filter_tap_coefficients.shape[0]
    rows_here = stereo_neuron_outputs.shape[1]
    cols_here = stereo_neuron_outputs.shape[3]
    hidden = extended_2(stereo_neuron_outputs, (("row", 1), ("col", 3)), layers_total)
    row_start = lax.axis_index("row") * rows_here
    col_start = lax.axis_index("col") * cols_here
    row_limit = lax.axis_size("row") * rows_here
    col_limit = lax.axis_size("col") * cols_here
    features = None
    for layer_number in range(layers_total):
        margin = layers_total - 1 - layer_number
        out_rows = rows_here + 2 * margin
        out_cols = cols_here + 2 * margin
        summed = None
        for tap_row in range(3):
            for tap_col in range(3):
                window = hidden[:, tap_row : tap_row + out_rows, :, tap_col : tap_col + out_cols]
                term = jnp.einsum(
                    "oc,iycx->iyox",
                    filter_tap_coefficients[layer_number, tap_row, tap_col],
                    window,
                    preferred_element_type=jnp.float32,
                )
                summed = term if summed is None else summed + term
        summed = summed + filter_stack_intercepts[layer_number][None, None, :, None]
        if layer_number < layers_total - 1:
            global_rows = row_start - margin + jnp.arange(out_rows, dtype=jnp.int32)
            global_cols = col_start - margin + jnp.arange(out_cols, dtype=jnp.int32)
            keep_rows = jnp.logical_and(global_rows >= 0, global_rows < row_limit)
            keep_cols = jnp.logical_and(global_cols >= 0, global_cols < col_limit)
            keeper = jnp.logical_and(keep_rows[None, :, None, None], keep_cols[None, None, None, :])
            hidden = jnp.where(keeper, jnp.maximum(summed, 0.0), 0.0).astype(jnp.bfloat16)
        else:
            features = summed
    scale = lax.rsqrt(jnp.sum(features * features, axis=2, keepdims=True) + 1e-06)
    return (features * scale).astype(jnp.bfloat16)


def per_device(
    stereo_neuron_outputs,
    filter_tap_coefficients,
    filter_stack_intercepts,
    reference_picture_present,
    tile_shift_amounts,
    smoothness_charges,
):
    unit = conv_stack(stereo_neuron_outputs, filter_tap_coefficients, filter_stack_intercepts)
    left_unit = unit[0]
    right_normalized_features = unit[1]
    rows_here = left_unit.shape[0]
    cols_here = left_unit.shape[2]
    reach = (3 * cols_here + DISPARITIES - 2) // cols_here
    tile_offset = tile_shift_amounts[0, 0]
    banded = lax.all_gather(right_normalized_features, "col", axis=2, tiled=True)
    filler = jnp.zeros(
        (rows_here, right_normalized_features.shape[1], reach * cols_here), jnp.bfloat16
    )
    extended = jnp.concatenate([filler, banded], axis=2)
    strip_start = (
        lax.axis_index("col") * cols_here + reach * cols_here - tile_offset - (DISPARITIES - 1)
    )
    strip = lax.dynamic_slice_in_dim(extended, strip_start, cols_here + DISPARITIES - 1, 2)
    product = jnp.einsum("ycj,yck->yjk", left_unit, strip, preferred_element_type=jnp.float32)
    padded = jnp.pad(product, ((0, 0), (0, 0), (0, 1)))
    flat = padded.reshape(rows_here, cols_here * (cols_here + DISPARITIES))
    flat = jnp.pad(flat, ((0, 0), (0, cols_here)))
    skewed = flat.reshape(rows_here, cols_here, cols_here + DISPARITIES + 1)[:, :, :DISPARITIES]
    similarity = skewed[:, :, ::-1]
    cost = jnp.where(reference_picture_present[:, :, None] == 1, 1.0 - similarity, 1.0)
    gentle_change_charge = smoothness_charges[0].astype(jnp.float32) / 64.0
    steep_change_charge = smoothness_charges[1].astype(jnp.float32) / 64.0
    across = jnp.swapaxes(cost, 0, 1)
    column_edge = jnp.zeros((cols_here // BLOCKS, DISPARITIES), jnp.float32)
    row_edge = jnp.zeros((rows_here // BLOCKS, DISPARITIES), jnp.float32)
    start_vertical = (column_edge, column_edge, jnp.zeros_like(cost))
    start_horizontal = (row_edge, row_edge, jnp.zeros_like(across))
    vertical_done = lax.fori_loop(
        0,
        lax.axis_size("row") + BLOCKS - 1,
        lambda turn, carry: vertical_turn(
            turn, carry, cost, gentle_change_charge, steep_change_charge
        ),
        start_vertical,
    )
    horizontal_done = lax.fori_loop(
        0,
        lax.axis_size("col") + BLOCKS - 1,
        lambda turn, carry: horizontal_turn(
            turn, carry, across, gentle_change_charge, steep_change_charge
        ),
        start_horizontal,
    )
    vertical = vertical_done[2]
    horizontal = horizontal_done[2]
    return vertical + jnp.swapaxes(horizontal, 0, 1)


def solution(mesh):
    return jax.shard_map(
        per_device,
        mesh=mesh,
        in_specs=(P(None, "row", None, "col"), P(), P(), P("row", "col"), P("row", "col"), P()),
        out_specs=P("row", "col", None),
        check_vma=False,
    )
```

profile of v0, /device:TPU:0, one launch (start us, length us, event | category | flops | bytes accessed | tf_op | source)
XLA Modules:
  0.0 408.0 jit_solution(13665944224499316811)
XLA Ops:
  1.0 4.8 %collective-permute-start.4 = (bf16[2,3,64,128]{3,2,1,0:T(8,128)(2,1)S(1)}, bf16[2,3,64,128]{3,2,1,0:T(8,128)(2,1)S(1)}, u32[]{:S(2)}, u32[]{:S(2)}) collective-permute-start(bf16[2,3,64,128]{3,2,1,0:T(8,128)(2,1)S(1)} %get-tuple-element.874), channel_id=1, source_target_pairs={{0,4},{4,8},{8,12},{12,16},{16,20},{20,24},{24,28},{1,5},{5,9},{9,... | collective-permute-start | bytes 294920 | tf_op jit(solution)/shard_map/ppermute | solution.py:23
  30.4 12.1 %all-gather = bf16[1,8,64,512]{3,2,1,0:T(8,128)(2,1)S(1)} all-gather(bf16[1,8,64,128]{3,2,1,0:T(8,128)(2,1)S(1)} %slice.342), channel_id=2, replica_groups=mesh['row'=8,'col'=4] {'col'}, dimensions={3}, use_global_device_ids=true | all-gather | bytes 655360 | tf_op jit(solution)/shard_map/all_gather | solution.py:172
  46.6 253.2 %while.91 = (s32[]{:T(128)}, f32[4,128]{1,0:T(4,128)S(1)}, f32[4,128]{1,0:T(4,128)S(1)}, f32[128,8,128]{2,1,0:T(8,128)S(1)}, f32[128,8,128]{2,1,0:T(8,128)S(1)},...) while((s32[]{:T(128)}, f32[4,128]{1,0:T(4,128)S(1)}, ...), condition=%wide.region_24.25_spmd, body=%wide.region_13.24_spmd.sunk | while | flops 138272 | bytes 2956247 | solution.py:203
  50.1 37.1 %conditional.10 = ((f32[4,128]{1,0:T(4,128)S(1)}, f32[128,8,128]{2,1,0:T(8,128)S(1)})) conditional(s32[]{:T(128)} %convert_element_type.108, (f32[4,128]{1,0:T(4,128)S(1)}, f32[128,8,128]{2,1,0:T(8,128)S(1)}) %tuple.201, (s32[]{:T(128)}, f32[128,8,128]{2,1,0:T(8,128)S(1)}, f32[]{:T(128)}, f32[]{:T(128)}, f32[4,128]{1,0:T(4,128)S(1)}, ...), branch_computations={%region_14.14_spmd, %region_15.18_spmd} | conditional | flops 69128 | bytes 1334531 | solution.py:65
  50.1 36.9 %while.88 = (s32[]{:T(128)}, f32[4,128]{1,0:T(4,128)S(1)}, f32[128,4,128]{2,1,0:T(4,128)S(1)}, f32[128,4,128]{2,1,0:T(4,128)S(1)}, f32[]{:T(128)}, /*index=5*/f32[]{:T(128)}, s32[]{:T(128)}, f32[]{:T(128)}) while((s32[]{:T(128)}, f32[4,128]{1,0:T(4,128)S(1)}, f32[128,4,128]{2,1,0:T(4,128)S(1)}, f32[128,4,128]{2,1,0:T(4,128)S(1)}, ...), condition=%wide.region_18.17_spmd, body=%wide.region_16.16_spmd.sunk | while | flops 3586 | bytes 23637 | solution.py:47
  89.9 37.1 %conditional.10 = ((f32[4,128]{1,0:T(4,128)S(1)}, f32[128,8,128]{2,1,0:T(8,128)S(1)})) conditional(s32[]{:T(128)} %convert_element_type.108, (f32[4,128]{1,0:T(4,128)S(1)}, f32[128,8,128]{2,1,0:T(8,128)S(1)}) %tuple.201, (s32[]{:T(128)}, f32[128,8,128]{2,1,0:T(8,128)S(1)}, f32[]{:T(128)}, f32[]{:T(128)}, f32[4,128]{1,0:T(4,128)S(1)}, ...), branch_computations={%region_14.14_spmd, %region_15.18_spmd} | conditional | flops 69128 | bytes 1334531 | solution.py:65
  90.0 36.9 %while.88 = (s32[]{:T(128)}, f32[4,128]{1,0:T(4,128)S(1)}, f32[128,4,128]{2,1,0:T(4,128)S(1)}, f32[128,4,128]{2,1,0:T(4,128)S(1)}, f32[]{:T(128)}, /*index=5*/f32[]{:T(128)}, s32[]{:T(128)}, f32[]{:T(128)}) while((s32[]{:T(128)}, f32[4,128]{1,0:T(4,128)S(1)}, f32[128,4,128]{2,1,0:T(4,128)S(1)}, f32[128,4,128]{2,1,0:T(4,128)S(1)}, ...), condition=%wide.region_18.17_spmd, body=%wide.region_16.16_spmd.sunk | while | flops 3586 | bytes 23637 | solution.py:47
  127.1 3.0 collective-permute-start
  131.5 6.6 %collective-permute-done.1 = f32[4,128]{1,0:T(4,128)S(1)} collective-permute-done((f32[4,128]{1,0:T(4,128)S(1)}, f32[4,128]{1,0:T(4,128)S(1)}, u32[]{:S(2)}, u32[]{:S(2)}) %collective-permute-start.1) | collective-permute-done | bytes 2080 | tf_op jit(solution)/shard_map/while/body/eval_jaxpr/ppermute | solution.py:13
  138.2 75.7 %collective-permute-start = (f32[4,128]{1,0:T(4,128)S(1)}, f32[4,128]{1,0:T(4,128)S(1)}, u32[]{:S(2)}, u32[]{:S(2)}) collective-permute-start(f32[4,128]{1,0:T(4,128)S(1)} %get-tuple-element.1346), channel_id=1, source_target_pairs={{0,1},{1,2},{2,3},{4,5},{5,6},{6,7},{8,9},{9,10},{10,11},{12,13},{... | collective-permute-start | bytes 6152 | tf_op jit(solution)/shard_map/while/body/eval_jaxpr/ppermute | solution.py:13
  218.1 37.1 %conditional.11 = ((f32[4,128]{1,0:T(4,128)S(1)}, f32[128,8,128]{2,1,0:T(8,128)S(1)})) conditional(s32[]{:T(128)} %convert_element_type.109, (f32[4,128]{1,0:T(4,128)S(1)}, f32[128,8,128]{2,1,0:T(8,128)S(1)}) %tuple.203, (s32[]{:T(128)}, f32[128,8,128]{2,1,0:T(8,128)S(1)}, f32[]{:T(128)}, f32[]{:T(128)}, f32[4,128]{1,0:T(4,128)S(1)}, ...), branch_computations={%region_19.19_spmd, %region_20.23_spmd} | conditional | flops 69129 | bytes 1596707 | solution.py:65
  218.2 36.9 %while.89 = (s32[]{:T(128)}, f32[4,128]{1,0:T(4,128)S(1)}, f32[128,4,128]{2,1,0:T(4,128)S(1)}, f32[128,4,128]{2,1,0:T(4,128)S(1)}, f32[]{:T(128)}, /*index=5*/f32[]{:T(128)}, s32[]{:T(128)}, s32[]{:T(128)}, f32[]{:T(128)}) while((s32[]{:T(128)}, f32[4,128]{1,0:T(4,128)S(1)}, f32[128,4,128]{2,1,0:T(4,128)S(1)}, ...), condition=%wide.region_23.22_spmd, body=%wide.region_21.21_spmd.sunk | while | flops 3587 | bytes 23657 | solution.py:47
  255.3 4.3 %collective-permute-start = (f32[4,128]{1,0:T(4,128)S(1)}, f32[4,128]{1,0:T(4,128)S(1)}, u32[]{:S(2)}, u32[]{:S(2)}) collective-permute-start(f32[4,128]{1,0:T(4,128)S(1)} %get-tuple-element.1346), channel_id=1, source_target_pairs={{0,1},{1,2},{2,3},{4,5},{5,6},{6,7},{8,9},{9,10},{10,11},{12,13},{... | collective-permute-start | bytes 6152 | tf_op jit(solution)/shard_map/while/body/eval_jaxpr/ppermute | solution.py:13
  262.6 37.1 %conditional.11 = ((f32[4,128]{1,0:T(4,128)S(1)}, f32[128,8,128]{2,1,0:T(8,128)S(1)})) conditional(s32[]{:T(128)} %convert_element_type.109, (f32[4,128]{1,0:T(4,128)S(1)}, f32[128,8,128]{2,1,0:T(8,128)S(1)}) %tuple.203, (s32[]{:T(128)}, f32[128,8,128]{2,1,0:T(8,128)S(1)}, f32[]{:T(128)}, f32[]{:T(128)}, f32[4,128]{1,0:T(4,128)S(1)}, ...), branch_computations={%region_19.19_spmd, %region_20.23_spmd} | conditional | flops 69129 | bytes 1596707 | solution.py:65
  262.7 36.9 %while.89 = (s32[]{:T(128)}, f32[4,128]{1,0:T(4,128)S(1)}, f32[128,4,128]{2,1,0:T(4,128)S(1)}, f32[128,4,128]{2,1,0:T(4,128)S(1)}, f32[]{:T(128)}, /*index=5*/f32[]{:T(128)}, s32[]{:T(128)}, s32[]{:T(128)}, f32[]{:T(128)}) while((s32[]{:T(128)}, f32[4,128]{1,0:T(4,128)S(1)}, f32[128,4,128]{2,1,0:T(4,128)S(1)}, ...), condition=%wide.region_23.22_spmd, body=%wide.region_21.21_spmd.sunk | while | flops 3587 | bytes 23657 | solution.py:47
  299.9 107.2 %while.90 = (s32[]{:T(128)}, f32[64,128]{1,0:T(8,128)S(1)}, f32[64,128]{1,0:T(8,128)S(1)}, f32[8,128,128]{2,1,0:T(8,128)S(1)}, f32[8,128,128]{2,1,0:T(8,128)S(1)...) while((s32[]{:T(128)}, f32[64,128]{1,0:T(8,128)S(1)}, ...), condition=%wide.region_12.13_spmd, body=%wide.region_1.12_spmd.sunk | while | flops 294817 | bytes 3999763 | solution.py:195
  299.9 4.3 %collective-permute-start.2 = (bf16[64,128]{1,0:T(8,128)(2,1)S(1)}, bf16[64,128]{1,0:T(8,128)(2,1)S(1)}, u32[]{:S(2)}, u32[]{:S(2)}) collective-permute-start(bf16[64,128]{1,0:T(8,128)(2,1)S(1)} %convert_element_type.103), channel_id=1, source_target_pairs={{0,4},{4,8},{8,12},{12,16},{16,20},{20,24},{24,28},{1,5},{5,9},{9,... | collective-permute-start | bytes 49160 | tf_op jit(solution)/shard_map/while/body/eval_jaxpr/ppermute | solution.py:13
  309.9 3.4 collective-permute-start.2
  319.0 4.3 %collective-permute-start.2 = (bf16[64,128]{1,0:T(8,128)(2,1)S(1)}, bf16[64,128]{1,0:T(8,128)(2,1)S(1)}, u32[]{:S(2)}, u32[]{:S(2)}) collective-permute-start(bf16[64,128]{1,0:T(8,128)(2,1)S(1)} %convert_element_type.103), channel_id=1, source_target_pairs={{0,4},{4,8},{8,12},{12,16},{16,20},{20,24},{24,28},{1,5},{5,9},{9,... | collective-permute-start | bytes 49160 | tf_op jit(solution)/shard_map/while/body/eval_jaxpr/ppermute | solution.py:13
  324.8 4.2 %collective-permute-done.3 = bf16[64,128]{1,0:T(8,128)(2,1)S(1)} collective-permute-done((bf16[64,128]{1,0:T(8,128)(2,1)S(1)}, bf16[64,128]{1,0:T(8,128)(2,1)S(1)}, u32[]{:S(2)}, u32[]{:S(2)}) %collective-permute-start.3) | collective-permute-done | bytes 16416 | tf_op jit(solution)/shard_map/while/body/eval_jaxpr/ppermute | solution.py:13
  329.0 3.4 collective-permute-start.2
  333.9 4.2 %collective-permute-done.3 = bf16[64,128]{1,0:T(8,128)(2,1)S(1)} collective-permute-done((bf16[64,128]{1,0:T(8,128)(2,1)S(1)}, bf16[64,128]{1,0:T(8,128)(2,1)S(1)}, u32[]{:S(2)}, u32[]{:S(2)}) %collective-permute-start.3) | collective-permute-done | bytes 16416 | tf_op jit(solution)/shard_map/while/body/eval_jaxpr/ppermute | solution.py:13
  338.1 4.4 %collective-permute-start.2 = (bf16[64,128]{1,0:T(8,128)(2,1)S(1)}, bf16[64,128]{1,0:T(8,128)(2,1)S(1)}, u32[]{:S(2)}, u32[]{:S(2)}) collective-permute-start(bf16[64,128]{1,0:T(8,128)(2,1)S(1)} %convert_element_type.103), channel_id=1, source_target_pairs={{0,4},{4,8},{8,12},{12,16},{16,20},{20,24},{24,28},{1,5},{5,9},{9,... | collective-permute-start | bytes 49160 | tf_op jit(solution)/shard_map/while/body/eval_jaxpr/ppermute | solution.py:13
  343.9 4.2 %collective-permute-done.3 = bf16[64,128]{1,0:T(8,128)(2,1)S(1)} collective-permute-done((bf16[64,128]{1,0:T(8,128)(2,1)S(1)}, bf16[64,128]{1,0:T(8,128)(2,1)S(1)}, u32[]{:S(2)}, u32[]{:S(2)}) %collective-permute-start.3) | collective-permute-done | bytes 16416 | tf_op jit(solution)/shard_map/while/body/eval_jaxpr/ppermute | solution.py:13
  348.1 6.0 %collective-permute-start.2 = (bf16[64,128]{1,0:T(8,128)(2,1)S(1)}, bf16[64,128]{1,0:T(8,128)(2,1)S(1)}, u32[]{:S(2)}, u32[]{:S(2)}) collective-permute-start(bf16[64,128]{1,0:T(8,128)(2,1)S(1)} %convert_element_type.103), channel_id=1, source_target_pairs={{0,4},{4,8},{8,12},{12,16},{16,20},{20,24},{24,28},{1,5},{5,9},{9,... | collective-permute-start | bytes 49160 | tf_op jit(solution)/shard_map/while/body/eval_jaxpr/ppermute | solution.py:13
  355.5 6.9 %collective-permute-done.3 = bf16[64,128]{1,0:T(8,128)(2,1)S(1)} collective-permute-done((bf16[64,128]{1,0:T(8,128)(2,1)S(1)}, bf16[64,128]{1,0:T(8,128)(2,1)S(1)}, u32[]{:S(2)}, u32[]{:S(2)}) %collective-permute-start.3) | collective-permute-done | bytes 16416 | tf_op jit(solution)/shard_map/while/body/eval_jaxpr/ppermute | solution.py:13
  362.5 7.6 %collective-permute-start.2 = (bf16[64,128]{1,0:T(8,128)(2,1)S(1)}, bf16[64,128]{1,0:T(8,128)(2,1)S(1)}, u32[]{:S(2)}, u32[]{:S(2)}) collective-permute-start(bf16[64,128]{1,0:T(8,128)(2,1)S(1)} %convert_element_type.103), channel_id=1, source_target_pairs={{0,4},{4,8},{8,12},{12,16},{16,20},{20,24},{24,28},{1,5},{5,9},{9,... | collective-permute-start | bytes 49160 | tf_op jit(solution)/shard_map/while/body/eval_jaxpr/ppermute | solution.py:13
  371.5 7.0 %collective-permute-done.3 = bf16[64,128]{1,0:T(8,128)(2,1)S(1)} collective-permute-done((bf16[64,128]{1,0:T(8,128)(2,1)S(1)}, bf16[64,128]{1,0:T(8,128)(2,1)S(1)}, u32[]{:S(2)}, u32[]{:S(2)}) %collective-permute-start.3) | collective-permute-done | bytes 16416 | tf_op jit(solution)/shard_map/while/body/eval_jaxpr/ppermute | solution.py:13
  378.5 7.6 %collective-permute-start.2 = (bf16[64,128]{1,0:T(8,128)(2,1)S(1)}, bf16[64,128]{1,0:T(8,128)(2,1)S(1)}, u32[]{:S(2)}, u32[]{:S(2)}) collective-permute-start(bf16[64,128]{1,0:T(8,128)(2,1)S(1)} %convert_element_type.103), channel_id=1, source_target_pairs={{0,4},{4,8},{8,12},{12,16},{16,20},{20,24},{24,28},{1,5},{5,9},{9,... | collective-permute-start | bytes 49160 | tf_op jit(solution)/shard_map/while/body/eval_jaxpr/ppermute | solution.py:13
  387.6 4.2 %collective-permute-done.3 = bf16[64,128]{1,0:T(8,128)(2,1)S(1)} collective-permute-done((bf16[64,128]{1,0:T(8,128)(2,1)S(1)}, bf16[64,128]{1,0:T(8,128)(2,1)S(1)}, u32[]{:S(2)}, u32[]{:S(2)}) %collective-permute-start.3) | collective-permute-done | bytes 16416 | tf_op jit(solution)/shard_map/while/body/eval_jaxpr/ppermute | solution.py:13
  394.6 4.0 collective-permute-start.2
  400.1 4.2 %collective-permute-done.3 = bf16[64,128]{1,0:T(8,128)(2,1)S(1)} collective-permute-done((bf16[64,128]{1,0:T(8,128)(2,1)S(1)}, bf16[64,128]{1,0:T(8,128)(2,1)S(1)}, u32[]{:S(2)}, u32[]{:S(2)}) %collective-permute-start.3) | collective-permute-done | bytes 16416 | tf_op jit(solution)/shard_map/while/body/eval_jaxpr/ppermute | solution.py:13
  (2419 shorter events, 231.3 us)
Async XLA Ops:
  1.0 7.9 %collective-permute-start.4 = (bf16[2,3,64,128]{3,2,1,0:T(8,128)(2,1)S(1)}, bf16[2,3,64,128]{3,2,1,0:T(8,128)(2,1)S(1)}, u32[]{:S(2)}, u32[]{:S(2)}) collective-permute-start(bf16[2,3,64,128]{3,2,1,0:T(8,128)(2,1)S(1)} %get-tuple-element.874), channel_id=1, source_target_pairs={{0,4},{4,8},{8,12},{12,16},{16,20},{20,24},{24,28},{1,5},{5,9},{9,... | collective-permute-start | bytes 294920 | tf_op jit(solution)/shard_map/ppermute | solution.py:23
  5.8 6.5 %collective-permute-start.5 = (bf16[2,3,64,128]{3,2,1,0:T(8,128)(2,1)S(1)}, bf16[2,3,64,128]{3,2,1,0:T(8,128)(2,1)S(1)}, u32[]{:S(2)}, u32[]{:S(2)}) collective-permute-start(bf16[2,3,64,128]{3,2,1,0:T(8,128)(2,1)S(1)} %get-tuple-element.873), channel_id=1, source_target_pairs={{4,0},{8,4},{12,8},{16,12},{20,16},{24,20},{28,24},{5,1},{9,5},{13... | collective-permute-start | bytes 294920 | tf_op jit(solution)/shard_map/ppermute | solution.py:24
  12.6 5.2 %collective-permute-start.6 = (bf16[2,14,64,3]{3,2,1,0:T(8,128)(2,1)S(1)}, bf16[2,14,64,3]{3,2,1,0:T(8,128)(2,1)S(1)}, u32[]{:S(2)}, u32[]{:S(2)}) collective-permute-start(bf16[2,14,64,3]{3,2,1,0:T(8,128)(2,1)S(1)} %get-tuple-element.871), channel_id=1, source_target_pairs={{0,1},{1,2},{2,3},{4,5},{5,6},{6,7},{8,9},{9,10},{10,11},{12,13},{... | collective-permute-start | bytes 32264 | tf_op jit(solution)/shard_map/ppermute | solution.py:23
  14.1 5.4 %collective-permute-start.7 = (bf16[2,14,64,3]{3,2,1,0:T(8,128)(2,1)S(1)}, bf16[2,14,64,3]{3,2,1,0:T(8,128)(2,1)S(1)}, u32[]{:S(2)}, u32[]{:S(2)}) collective-permute-start(bf16[2,14,64,3]{3,2,1,0:T(8,128)(2,1)S(1)} %get-tuple-element.872), channel_id=1, source_target_pairs={{1,0},{2,1},{3,2},{5,4},{6,5},{7,6},{9,8},{10,9},{11,10},{13,12},{... | collective-permute-start | bytes 32264 | tf_op jit(solution)/shard_map/ppermute | solution.py:24
  46.6 3.4 collective-permute-start
  48.7 38.5 %collective-permute-start.1 = (f32[4,128]{1,0:T(4,128)S(1)}, f32[4,128]{1,0:T(4,128)S(1)}, u32[]{:S(2)}, u32[]{:S(2)}) collective-permute-start(f32[4,128]{1,0:T(4,128)S(1)} %get-tuple-element.1347), channel_id=1, source_target_pairs={{1,0},{2,1},{3,2},{5,4},{6,5},{7,6},{9,8},{10,9},{11,10},{13,12},{... | collective-permute-start | bytes 6152 | tf_op jit(solution)/shard_map/while/body/eval_jaxpr/ppermute | solution.py:13
  87.3 2.6 collective-permute-start
  88.6 38.5 %collective-permute-start.1 = (f32[4,128]{1,0:T(4,128)S(1)}, f32[4,128]{1,0:T(4,128)S(1)}, u32[]{:S(2)}, u32[]{:S(2)}) collective-permute-start(f32[4,128]{1,0:T(4,128)S(1)} %get-tuple-element.1347), channel_id=1, source_target_pairs={{1,0},{2,1},{3,2},{5,4},{6,5},{7,6},{9,8},{10,9},{11,10},{13,12},{... | collective-permute-start | bytes 6152 | tf_op jit(solution)/shard_map/while/body/eval_jaxpr/ppermute | solution.py:13
  127.1 4.4 %collective-permute-start = (f32[4,128]{1,0:T(4,128)S(1)}, f32[4,128]{1,0:T(4,128)S(1)}, u32[]{:S(2)}, u32[]{:S(2)}) collective-permute-start(f32[4,128]{1,0:T(4,128)S(1)} %get-tuple-element.1346), channel_id=1, source_target_pairs={{0,1},{1,2},{2,3},{4,5},{5,6},{6,7},{8,9},{9,10},{10,11},{12,13},{... | collective-permute-start | bytes 6152 | tf_op jit(solution)/shard_map/while/body/eval_jaxpr/ppermute | solution.py:13
  130.2 8.0 %collective-permute-start.1 = (f32[4,128]{1,0:T(4,128)S(1)}, f32[4,128]{1,0:T(4,128)S(1)}, u32[]{:S(2)}, u32[]{:S(2)}) collective-permute-start(f32[4,128]{1,0:T(4,128)S(1)} %get-tuple-element.1347), channel_id=1, source_target_pairs={{1,0},{2,1},{3,2},{5,4},{6,5},{7,6},{9,8},{10,9},{11,10},{13,12},{... | collective-permute-start | bytes 6152 | tf_op jit(solution)/shard_map/while/body/eval_jaxpr/ppermute | solution.py:13
  138.2 77.0 %collective-permute-start = (f32[4,128]{1,0:T(4,128)S(1)}, f32[4,128]{1,0:T(4,128)S(1)}, u32[]{:S(2)}, u32[]{:S(2)}) collective-permute-start(f32[4,128]{1,0:T(4,128)S(1)} %get-tuple-element.1346), channel_id=1, source_target_pairs={{0,1},{1,2},{2,3},{4,5},{5,6},{6,7},{8,9},{9,10},{10,11},{12,13},{... | collective-permute-start | bytes 6152 | tf_op jit(solution)/shard_map/while/body/eval_jaxpr/ppermute | solution.py:13
  213.8 4.3 %collective-permute-start.1 = (f32[4,128]{1,0:T(4,128)S(1)}, f32[4,128]{1,0:T(4,128)S(1)}, u32[]{:S(2)}, u32[]{:S(2)}) collective-permute-start(f32[4,128]{1,0:T(4,128)S(1)} %get-tuple-element.1347), channel_id=1, source_target_pairs={{1,0},{2,1},{3,2},{5,4},{6,5},{7,6},{9,8},{10,9},{11,10},{13,12},{... | collective-permute-start | bytes 6152 | tf_op jit(solution)/shard_map/while/body/eval_jaxpr/ppermute | solution.py:13
  255.3 5.6 %collective-permute-start = (f32[4,128]{1,0:T(4,128)S(1)}, f32[4,128]{1,0:T(4,128)S(1)}, u32[]{:S(2)}, u32[]{:S(2)}) collective-permute-start(f32[4,128]{1,0:T(4,128)S(1)} %get-tuple-element.1346), channel_id=1, source_target_pairs={{0,1},{1,2},{2,3},{4,5},{5,6},{6,7},{8,9},{9,10},{10,11},{12,13},{... | collective-permute-start | bytes 6152 | tf_op jit(solution)/shard_map/while/body/eval_jaxpr/ppermute | solution.py:13
  259.6 3.1 collective-permute-start.1
  299.9 5.8 %collective-permute-start.2 = (bf16[64,128]{1,0:T(8,128)(2,1)S(1)}, bf16[64,128]{1,0:T(8,128)(2,1)S(1)}, u32[]{:S(2)}, u32[]{:S(2)}) collective-permute-start(bf16[64,128]{1,0:T(8,128)(2,1)S(1)} %convert_element_type.103), channel_id=1, source_target_pairs={{0,4},{4,8},{8,12},{12,16},{16,20},{20,24},{24,28},{1,5},{5,9},{9,... | collective-permute-start | bytes 49160 | tf_op jit(solution)/shard_map/while/body/eval_jaxpr/ppermute | solution.py:13
  304.3 5.6 %collective-permute-start.3 = (bf16[64,128]{1,0:T(8,128)(2,1)S(1)}, bf16[64,128]{1,0:T(8,128)(2,1)S(1)}, u32[]{:S(2)}, u32[]{:S(2)}) collective-permute-start(bf16[64,128]{1,0:T(8,128)(2,1)S(1)} %convert_element_type.106), channel_id=1, source_target_pairs={{4,0},{8,4},{12,8},{16,12},{20,16},{24,20},{28,24},{5,1},{9,5},{13... | collective-permute-start | bytes 49160 | tf_op jit(solution)/shard_map/while/body/eval_jaxpr/ppermute | solution.py:13
  309.9 4.8 %collective-permute-start.2 = (bf16[64,128]{1,0:T(8,128)(2,1)S(1)}, bf16[64,128]{1,0:T(8,128)(2,1)S(1)}, u32[]{:S(2)}, u32[]{:S(2)}) collective-permute-start(bf16[64,128]{1,0:T(8,128)(2,1)S(1)} %convert_element_type.103), channel_id=1, source_target_pairs={{0,4},{4,8},{8,12},{12,16},{16,20},{20,24},{24,28},{1,5},{5,9},{9,... | collective-permute-start | bytes 49160 | tf_op jit(solution)/shard_map/while/body/eval_jaxpr/ppermute | solution.py:13
  313.4 5.6 %collective-permute-start.3 = (bf16[64,128]{1,0:T(8,128)(2,1)S(1)}, bf16[64,128]{1,0:T(8,128)(2,1)S(1)}, u32[]{:S(2)}, u32[]{:S(2)}) collective-permute-start(bf16[64,128]{1,0:T(8,128)(2,1)S(1)} %convert_element_type.106), channel_id=1, source_target_pairs={{4,0},{8,4},{12,8},{16,12},{20,16},{24,20},{28,24},{5,1},{9,5},{13... | collective-permute-start | bytes 49160 | tf_op jit(solution)/shard_map/while/body/eval_jaxpr/ppermute | solution.py:13
  319.0 5.8 %collective-permute-start.2 = (bf16[64,128]{1,0:T(8,128)(2,1)S(1)}, bf16[64,128]{1,0:T(8,128)(2,1)S(1)}, u32[]{:S(2)}, u32[]{:S(2)}) collective-permute-start(bf16[64,128]{1,0:T(8,128)(2,1)S(1)} %convert_element_type.103), channel_id=1, source_target_pairs={{0,4},{4,8},{8,12},{12,16},{16,20},{20,24},{24,28},{1,5},{5,9},{9,... | collective-permute-start | bytes 49160 | tf_op jit(solution)/shard_map/while/body/eval_jaxpr/ppermute | solution.py:13
  323.4 5.6 %collective-permute-start.3 = (bf16[64,128]{1,0:T(8,128)(2,1)S(1)}, bf16[64,128]{1,0:T(8,128)(2,1)S(1)}, u32[]{:S(2)}, u32[]{:S(2)}) collective-permute-start(bf16[64,128]{1,0:T(8,128)(2,1)S(1)} %convert_element_type.106), channel_id=1, source_target_pairs={{4,0},{8,4},{12,8},{16,12},{20,16},{24,20},{28,24},{5,1},{9,5},{13... | collective-permute-start | bytes 49160 | tf_op jit(solution)/shard_map/while/body/eval_jaxpr/ppermute | solution.py:13
  329.0 4.8 %collective-permute-start.2 = (bf16[64,128]{1,0:T(8,128)(2,1)S(1)}, bf16[64,128]{1,0:T(8,128)(2,1)S(1)}, u32[]{:S(2)}, u32[]{:S(2)}) collective-permute-start(bf16[64,128]{1,0:T(8,128)(2,1)S(1)} %convert_element_type.103), channel_id=1, source_target_pairs={{0,4},{4,8},{8,12},{12,16},{16,20},{20,24},{24,28},{1,5},{5,9},{9,... | collective-permute-start | bytes 49160 | tf_op jit(solution)/shard_map/while/body/eval_jaxpr/ppermute | solution.py:13
  332.4 5.6 %collective-permute-start.3 = (bf16[64,128]{1,0:T(8,128)(2,1)S(1)}, bf16[64,128]{1,0:T(8,128)(2,1)S(1)}, u32[]{:S(2)}, u32[]{:S(2)}) collective-permute-start(bf16[64,128]{1,0:T(8,128)(2,1)S(1)} %convert_element_type.106), channel_id=1, source_target_pairs={{4,0},{8,4},{12,8},{16,12},{20,16},{24,20},{28,24},{5,1},{9,5},{13... | collective-permute-start | bytes 49160 | tf_op jit(solution)/shard_map/while/body/eval_jaxpr/ppermute | solution.py:13
  338.1 5.8 %collective-permute-start.2 = (bf16[64,128]{1,0:T(8,128)(2,1)S(1)}, bf16[64,128]{1,0:T(8,128)(2,1)S(1)}, u32[]{:S(2)}, u32[]{:S(2)}) collective-permute-start(bf16[64,128]{1,0:T(8,128)(2,1)S(1)} %convert_element_type.103), channel_id=1, source_target_pairs={{0,4},{4,8},{8,12},{12,16},{16,20},{20,24},{24,28},{1,5},{5,9},{9,... | collective-permute-start | bytes 49160 | tf_op jit(solution)/shard_map/while/body/eval_jaxpr/ppermute | solution.py:13
  342.5 5.6 %collective-permute-start.3 = (bf16[64,128]{1,0:T(8,128)(2,1)S(1)}, bf16[64,128]{1,0:T(8,128)(2,1)S(1)}, u32[]{:S(2)}, u32[]{:S(2)}) collective-permute-start(bf16[64,128]{1,0:T(8,128)(2,1)S(1)} %convert_element_type.106), channel_id=1, source_target_pairs={{4,0},{8,4},{12,8},{16,12},{20,16},{24,20},{28,24},{5,1},{9,5},{13... | collective-permute-start | bytes 49160 | tf_op jit(solution)/shard_map/while/body/eval_jaxpr/ppermute | solution.py:13
  348.1 7.4 %collective-permute-start.2 = (bf16[64,128]{1,0:T(8,128)(2,1)S(1)}, bf16[64,128]{1,0:T(8,128)(2,1)S(1)}, u32[]{:S(2)}, u32[]{:S(2)}) collective-permute-start(bf16[64,128]{1,0:T(8,128)(2,1)S(1)} %convert_element_type.103), channel_id=1, source_target_pairs={{0,4},{4,8},{8,12},{12,16},{16,20},{20,24},{24,28},{1,5},{5,9},{9,... | collective-permute-start | bytes 49160 | tf_op jit(solution)/shard_map/while/body/eval_jaxpr/ppermute | solution.py:13
  354.1 8.3 %collective-permute-start.3 = (bf16[64,128]{1,0:T(8,128)(2,1)S(1)}, bf16[64,128]{1,0:T(8,128)(2,1)S(1)}, u32[]{:S(2)}, u32[]{:S(2)}) collective-permute-start(bf16[64,128]{1,0:T(8,128)(2,1)S(1)} %convert_element_type.106), channel_id=1, source_target_pairs={{4,0},{8,4},{12,8},{16,12},{20,16},{24,20},{28,24},{5,1},{9,5},{13... | collective-permute-start | bytes 49160 | tf_op jit(solution)/shard_map/while/body/eval_jaxpr/ppermute | solution.py:13
  362.5 9.0 %collective-permute-start.2 = (bf16[64,128]{1,0:T(8,128)(2,1)S(1)}, bf16[64,128]{1,0:T(8,128)(2,1)S(1)}, u32[]{:S(2)}, u32[]{:S(2)}) collective-permute-start(bf16[64,128]{1,0:T(8,128)(2,1)S(1)} %convert_element_type.103), channel_id=1, source_target_pairs={{0,4},{4,8},{8,12},{12,16},{16,20},{20,24},{24,28},{1,5},{5,9},{9,... | collective-permute-start | bytes 49160 | tf_op jit(solution)/shard_map/while/body/eval_jaxpr/ppermute | solution.py:13
  370.1 8.4 %collective-permute-start.3 = (bf16[64,128]{1,0:T(8,128)(2,1)S(1)}, bf16[64,128]{1,0:T(8,128)(2,1)S(1)}, u32[]{:S(2)}, u32[]{:S(2)}) collective-permute-start(bf16[64,128]{1,0:T(8,128)(2,1)S(1)} %convert_element_type.106), channel_id=1, source_target_pairs={{4,0},{8,4},{12,8},{16,12},{20,16},{24,20},{28,24},{5,1},{9,5},{13... | collective-permute-start | bytes 49160 | tf_op jit(solution)/shard_map/while/body/eval_jaxpr/ppermute | solution.py:13
  378.5 9.0 %collective-permute-start.2 = (bf16[64,128]{1,0:T(8,128)(2,1)S(1)}, bf16[64,128]{1,0:T(8,128)(2,1)S(1)}, u32[]{:S(2)}, u32[]{:S(2)}) collective-permute-start(bf16[64,128]{1,0:T(8,128)(2,1)S(1)} %convert_element_type.103), channel_id=1, source_target_pairs={{0,4},{4,8},{8,12},{12,16},{16,20},{20,24},{24,28},{1,5},{5,9},{9,... | collective-permute-start | bytes 49160 | tf_op jit(solution)/shard_map/while/body/eval_jaxpr/ppermute | solution.py:13
  386.2 5.6 %collective-permute-start.3 = (bf16[64,128]{1,0:T(8,128)(2,1)S(1)}, bf16[64,128]{1,0:T(8,128)(2,1)S(1)}, u32[]{:S(2)}, u32[]{:S(2)}) collective-permute-start(bf16[64,128]{1,0:T(8,128)(2,1)S(1)} %convert_element_type.106), channel_id=1, source_target_pairs={{4,0},{8,4},{12,8},{16,12},{20,16},{24,20},{28,24},{5,1},{9,5},{13... | collective-permute-start | bytes 49160 | tf_op jit(solution)/shard_map/while/body/eval_jaxpr/ppermute | solution.py:13
  394.6 5.4 %collective-permute-start.2 = (bf16[64,128]{1,0:T(8,128)(2,1)S(1)}, bf16[64,128]{1,0:T(8,128)(2,1)S(1)}, u32[]{:S(2)}, u32[]{:S(2)}) collective-permute-start(bf16[64,128]{1,0:T(8,128)(2,1)S(1)} %convert_element_type.103), channel_id=1, source_target_pairs={{0,4},{4,8},{8,12},{12,16},{16,20},{20,24},{24,28},{1,5},{5,9},{9,... | collective-permute-start | bytes 49160 | tf_op jit(solution)/shard_map/while/body/eval_jaxpr/ppermute | solution.py:13
  398.7 5.6 %collective-permute-start.3 = (bf16[64,128]{1,0:T(8,128)(2,1)S(1)}, bf16[64,128]{1,0:T(8,128)(2,1)S(1)}, u32[]{:S(2)}, u32[]{:S(2)}) collective-permute-start(bf16[64,128]{1,0:T(8,128)(2,1)S(1)} %convert_element_type.106), channel_id=1, source_target_pairs={{4,0},{8,4},{12,8},{16,12},{20,16},{24,20},{28,24},{5,1},{9,5},{13... | collective-permute-start | bytes 49160 | tf_op jit(solution)/shard_map/while/body/eval_jaxpr/ppermute | solution.py:13
  (2 other events, 22.8 us)
where the time goes:
time: 409 us; the launch traced here: 408 us
  starting transfers between devices  158 us (39%)
  other arithmetic  114 us (28%)
  waiting for transfers between devices  54.2 us (13%)
  local copies, waits for them, and re-layouts  47.1 us (12%)
  blocking collectives  12.1 us (3%)
  matrix products  10.5 us (3%)
  loops' own time  8.96 us (2%)
    ppermute x28, starting transfers between devices, from_behind(): return lax.ppermute(block, axis, route)  150 us
    reduce_min x548, other arithmetic, advance(): least = jnp.min(state, axis=-1, keepdims=True)  68.7 us
    ppermute x28, waiting for transfers between devices, from_behind(): return lax.ppermute(block, axis, route)  50 us
    dynamic_update_slice x512, other arithmetic, sweep(): return lax.scan(stepper, incoming, costs, reverse=backward)  39.6 us
    slice x544, local copies, waits for them, and re-layouts, advance(): lower = jnp.concatenate([barrier, state[..., :-1]], axis=-1)  39.6 us
    all_gather x1, blocking collectives, per_device(): lax.all_gather(right_normalized_features, 'col', axis=2, tiled=True)  12.1 us
    dot_general x27, matrix products, conv_stack(): jnp.einsum('oc,iycx->iyox', filter_tap_coefficients[layer_number, tap_row...  10.1 us
  transfers between devices with their start and end apart: 32, of which 23 were waited for; matrix products, arithmetic and copies ran while one was open for 19% of the time, Pallas kernels for 0%

commit v1 on v0

v1 whole, which is shorter than its diff:
```python
import functools

import jax
import jax.numpy as jnp
from jax import lax
from jax.experimental import pallas as pl
from jax.experimental.pallas import tpu as pltpu
from jax.sharding import PartitionSpec as P

DISPARITIES = 128
OFF_MOST = 256
SUB = 8
REGS = DISPARITIES // SUB
VMEM_LIMIT = 56 * 1024 * 1024


def lane_to_disparity(lane):
    return (lane % SUB) * REGS + lane // SUB


def disparity_to_lane(disparity):
    return (disparity % REGS) * SUB + disparity // REGS


def advance(state, cost, p1, p2):
    lanes = state[0].shape[1]
    row = lax.broadcasted_iota(jnp.int32, (SUB, lanes), 0)
    below = jnp.where(row == 0, jnp.inf, pltpu.roll(state[-1], 1, 0))
    above = jnp.where(row == SUB - 1, jnp.inf, pltpu.roll(state[0], SUB - 1, 0))
    least = list(state)
    while len(least) > 1:
        least = [jnp.minimum(a, b) for a, b in zip(least[::2], least[1::2])]
    least = least[0]
    for turn in (4, 2, 1):
        least = jnp.minimum(least, pltpu.roll(least, turn, 0))
    lower = [below] + state[:-1]
    upper = state[1:] + [above]
    fresh = []
    for s, l, u, c in zip(state, lower, upper, cost):
        t = jnp.minimum(s, jnp.minimum(l, u) + p1)
        fresh.append(c + jnp.minimum(t - least, p2))
    return fresh


def charges(charge_ref):
    return (
        charge_ref[0].astype(jnp.float32) * (1.0 / 64.0),
        charge_ref[1].astype(jnp.float32) * (1.0 / 64.0),
    )


def registers(array):
    return [array[SUB * v : SUB * (v + 1)] for v in range(REGS)]


def band_kernel(
    place_ref, given_ref, filter_ref, bias_ref, cost_ref, own_ref,
    maps_a, maps_b, left_unit, right_unit, present,
):
    parts, _, channels, width = given_ref.shape
    layers = filter_ref.shape[0]
    rows = own_ref.shape[0]
    cols = parts * width
    high = rows + 2 * layers
    first_row = place_ref[0] * rows
    rows_total = place_ref[1] * rows
    own = place_ref[2]
    lead = (OFF_MOST + 2 * width - 1) // width * width

    for p in range(parts):
        present[:, p * width : (p + 1) * width] = given_ref[p, 2 * high, 0:16, :].astype(
            jnp.float32
        )
    right_unit[:, 0:lead] = jnp.zeros((rows * channels, lead), jnp.bfloat16)
    right_unit[:, lead + cols :] = jnp.zeros((rows * channels, width), jnp.bfloat16)

    column = lax.broadcasted_iota(jnp.int32, (1, cols), 1)
    for image in range(2):

        @pl.loop(0, high)
        def _(row):
            for p in range(parts):
                maps_a[pl.ds(pl.multiple_of(row * channels, channels), channels),
                       p * width : (p + 1) * width] = given_ref[p, image * high + row]

        for layer in range(layers):
            source, target = (maps_a, maps_b) if layer % 2 == 0 else (maps_b, maps_a)
            margin = layers - 1 - layer

            @pl.loop(0, rows + 2 * margin, unroll=2)
            def _(row):
                start = pl.multiple_of(row * channels, channels)
                window = source[pl.ds(start, 3 * channels), :]
                taps = jnp.dot(filter_ref[layer], window, preferred_element_type=jnp.float32)
                before = pltpu.roll(taps[:channels], 1, 1)
                after = pltpu.roll(taps[2 * channels :], cols - 1, 1)
                z = taps[channels : 2 * channels] + jnp.where(column == 0, 0.0, before)
                z = z + jnp.where(column == cols - 1, 0.0, after) + bias_ref[layer]
                if layer < layers - 1:
                    there = first_row - margin + row
                    inside = jnp.logical_and(there >= 0, there < rows_total)
                    z = jnp.maximum(z, 0.0) * jnp.where(inside, 1.0, 0.0)
                    target[pl.ds(start, channels), :] = z.astype(jnp.bfloat16)
                else:
                    scale = lax.rsqrt(jnp.sum(z * z, axis=0, keepdims=True) + 1e-06)
                    unit = (z * scale).astype(jnp.bfloat16)
                    if image == 0:
                        seen = present[pl.ds(row, 1), :]
                        unit = jnp.where(seen > 0.5, unit.astype(jnp.float32), 0.0)
                        left_unit[pl.ds(start, channels), :] = unit.astype(jnp.bfloat16)
                    else:
                        right_unit[pl.ds(start, channels), lead : lead + cols] = unit

    lane = lax.broadcasted_iota(jnp.int32, (width, DISPARITIES), 1)
    place = lax.broadcasted_iota(jnp.int32, (width, DISPARITIES), 0)

    @pl.loop(0, parts)
    def _(p):
        shift_block = given_ref[p, 2 * high, 16:32, :].astype(jnp.float32)
        shift = jnp.max(shift_block).astype(jnp.int32)
        base = p * width - shift + lead
        block = base // width
        ahead = place + (base - block * width)
        index = (ahead - lane_to_disparity(lane)) & (DISPARITIES - 1)
        start = pl.multiple_of((block - 1) * width, width)
        here = pl.multiple_of(p * width, width)
        for y in range(rows):
            left = left_unit[y * channels : (y + 1) * channels, pl.ds(here, width)]
            right = right_unit[y * channels : (y + 1) * channels, pl.ds(start, 3 * width)]
            product = lax.dot_general(
                left, right, (((0,), (0,)), ((), ())), preferred_element_type=jnp.float32
            )
            chosen = jnp.where(lane <= ahead, product[:, width : 2 * width], product[:, :width])
            chosen = jnp.where(lane <= ahead - width, product[:, 2 * width :], chosen)
            chosen = 1.0 - jnp.take_along_axis(chosen, index, axis=1, mode="promise_in_bounds")
            cost_ref[pl.ds(here, width), y, :] = chosen

            @pl.when(p == own)
            def _():
                own_ref[y] = chosen.T.astype(jnp.bfloat16)


def across_kernel(place_ref, charge_ref, cost_ref, kept_ref):
    cols, rows, _ = cost_ref.shape
    width = kept_ref.shape[0]
    parts = cols // width
    own = place_ref[2]
    p1, p2 = charges(charge_ref)

    def step(i, state, keep, first_col, last_col):
        right = cost_ref[first_col + i]
        left = cost_ref[last_col - i]
        cost = jnp.concatenate([right, left], axis=0).T
        fresh = advance(list(state), registers(cost), p1, p2)
        if keep:
            back = jnp.concatenate(fresh, axis=0).T
            kept_ref[i, 0:rows] = back[0:rows]
            kept_ref[width - 1 - i, rows : 2 * rows] = back[rows : 2 * rows]
        return tuple(fresh)

    state = tuple(jnp.zeros((SUB, 2 * rows), jnp.float32) for _ in range(REGS))

    def segment(p, state):
        first_col = p * width
        last_col = cols - 1 - p * width

        def plain(state):
            return lax.fori_loop(
                0, width, lambda i, s: step(i, s, False, first_col, last_col), state, unroll=8
            )

        def keeping(state):
            def body(i, s):
                right = cost_ref[first_col + i]
                left = cost_ref[last_col - i]
                cost = jnp.concatenate([right, left], axis=0).T
                fresh = advance(list(s), registers(cost), p1, p2)
                back = jnp.concatenate(fresh, axis=0).T

                @pl.when(p == own)
                def _():
                    kept_ref[i, 0:rows] = back[0:rows]

                @pl.when(parts - 1 - p == own)
                def _():
                    kept_ref[width - 1 - i, rows : 2 * rows] = back[rows : 2 * rows]

                return tuple(fresh)

            return lax.fori_loop(0, width, body, state, unroll=8)

        mine = jnp.logical_or(p == own, parts - 1 - p == own)
        return lax.cond(mine, keeping, plain, state)

    lax.fori_loop(0, parts, segment, state)


def down_or_up(forward, first_own, cost_ref, state, p1, p2, keep):
    group, rows = cost_ref.shape[:2]
    count = group * rows

    def body(i, state):
        row = jnp.where(forward, i, count - 1 - i)
        block = row // rows
        inner = row - block * rows
        cost = cost_ref[block, inner].astype(jnp.float32)
        fresh = advance(list(state), registers(cost), p1, p2)

        @pl.when(block == first_own)
        def _():
            keep(inner, jnp.concatenate(fresh, axis=0))

        return tuple(fresh)

    return lax.fori_loop(0, count, body, state, unroll=4)


def first_vertical_kernel(place_ref, charge_ref, cost_ref, kept_ref, last_ref):
    p1, p2 = charges(charge_ref)
    width = cost_ref.shape[-1]
    state = tuple(jnp.zeros((SUB, width), jnp.float32) for _ in range(REGS))

    def keep(row, value):
        kept_ref[row] = value

    final = down_or_up(place_ref[3] == 0, place_ref[4], cost_ref, state, p1, p2, keep)
    last_ref[...] = jnp.concatenate(final, axis=0).astype(jnp.bfloat16)


def second_vertical_kernel(
    place_ref, charge_ref, cost_ref, kept_ref, came_ref, across_ref, out_ref, total
):
    p1, p2 = charges(charge_ref)
    rows, _, width = kept_ref.shape
    state = tuple(registers(came_ref[...].astype(jnp.float32)))

    def keep(row, value):
        total[row] = value + kept_ref[row]

    down_or_up(place_ref[3] != 0, place_ref[4], cost_ref, state, p1, p2, keep)
    lane = lax.broadcasted_iota(jnp.int32, (width, DISPARITIES), 1)
    index = disparity_to_lane(lane)
    for row in range(rows):
        value = total[row].T + (across_ref[:, row, :] + across_ref[:, rows + row, :])
        out_ref[row] = jnp.take_along_axis(value, index, axis=1, mode="promise_in_bounds")


SMEM = functools.partial(pl.BlockSpec, memory_space=pltpu.SMEM)
VMEM = functools.partial(pl.BlockSpec, memory_space=pltpu.VMEM)


def call(kernel, outs, specs, scratch=(), flops=0):
    return pl.pallas_call(
        kernel,
        out_shape=outs,
        in_specs=specs,
        out_specs=jax.tree.map(lambda _: VMEM(), outs),
        scratch_shapes=list(scratch),
        compiler_params=pltpu.CompilerParams(vmem_limit_bytes=VMEM_LIMIT),
        cost_estimate=pl.CostEstimate(flops=flops, bytes_accessed=1 << 22, transcendentals=0),
    )


def per_device(activations, filters, biases, present, shifts, smooth):
    _, rows, channels, width = activations.shape
    layers = filters.shape[0]
    high = rows + 2 * layers
    row_rank, row_count = lax.axis_index("row"), lax.axis_size("row")
    col_rank, parts = lax.axis_index("col"), lax.axis_size("col")
    half = row_count // 2
    cols = parts * width
    place = jnp.stack(
        [row_rank, jnp.int32(row_count), col_rank, row_rank // half, row_rank % half]
    ).astype(jnp.int32)

    downward = [(i, i + 1) for i in range(row_count - 1)]
    upward = [(i + 1, i) for i in range(row_count - 1)]
    before = lax.ppermute(activations[:, rows - layers :], "row", downward)
    after = lax.ppermute(activations[:, :layers], "row", upward)
    extra = jnp.concatenate(
        [
            present.astype(jnp.bfloat16),
            jnp.zeros((16 - rows, width), jnp.bfloat16),
            jnp.broadcast_to(shifts.astype(jnp.bfloat16), (channels - 16, width)),
        ],
        axis=0,
    )
    block = jnp.concatenate([before, activations, after], axis=1)
    block = jnp.concatenate([block.reshape(2 * high, channels, width), extra[None]], axis=0)
    given = lax.all_gather(block, "col", axis=0)
    taps = jnp.transpose(filters, (0, 2, 3, 1, 4)).reshape(layers, 3 * channels, 3 * channels)

    f32, bf16 = jnp.float32, jnp.bfloat16
    lead = (OFF_MOST + 2 * width - 1) // width * width
    cost, own = call(
        band_kernel,
        (
            jax.ShapeDtypeStruct((cols, rows, DISPARITIES), f32),
            jax.ShapeDtypeStruct((rows, DISPARITIES, width), bf16),
        ),
        [SMEM(), VMEM(), VMEM(), VMEM()],
        [
            pltpu.VMEM((high * channels, cols), bf16),
            pltpu.VMEM(((high - 2) * channels, cols), bf16),
            pltpu.VMEM((rows * channels, cols), bf16),
            pltpu.VMEM((rows * channels, lead + cols + width), bf16),
            pltpu.VMEM((16, cols), f32),
        ],
        flops=10**10,
    )(place, given, taps, biases[:, :, None])

    groups = [list(range(half)), list(range(half, row_count))]
    gathered = lax.all_gather(own, "row", axis=0, axis_index_groups=groups)

    across = call(
        across_kernel,
        jax.ShapeDtypeStruct((width, 2 * rows, DISPARITIES), f32),
        [SMEM(), SMEM(), VMEM()],
        flops=2 * 10**10,
    )(place, smooth, cost)

    kept, last = call(
        first_vertical_kernel,
        (
            jax.ShapeDtypeStruct((rows, DISPARITIES, width), f32),
            jax.ShapeDtypeStruct((DISPARITIES, width), bf16),
        ),
        [SMEM(), SMEM(), VMEM()],
        flops=2 * 10**9,
    )(place, smooth, gathered)

    swap = [(i, (i + half) % row_count) for i in range(row_count)]
    came = lax.ppermute(last, "row", swap)

    return call(
        second_vertical_kernel,
        jax.ShapeDtypeStruct((rows, width, DISPARITIES), f32),
        [SMEM(), SMEM(), VMEM(), VMEM(), VMEM(), VMEM()],
        [pltpu.VMEM((rows, DISPARITIES, width), f32)],
        flops=3 * 10**9,
    )(place, smooth, gathered, kept, came, across)


def solution(mesh):
    return jax.shard_map(
        per_device,
        mesh=mesh,
        in_specs=(P(None, "row", None, "col"), P(), P(), P("row", "col"), P("row", "col"), P()),
        out_specs=P("row", "col", None),
        check_vma=False,
    )
```

time: 409 us -> 160 us (0.39)
  starting transfers between devices: 158 us -> 8.59 us
  other arithmetic: 114 us -> 2.6 us
  Pallas kernels: 0 us -> 78.9 us
  local copies, waits for them, and re-layouts: 47.1 us -> 4.66 us
  blocking collectives: 12.1 us -> 0 us
  between operations: 2.33 us -> 14.2 us
  matrix products: 10.5 us -> 0 us
  loops' own time: 8.96 us -> 0 us
    ppermute x32 -> x3, starting transfers between devices: 158 us -> 8.55 us  [the longest x1 4.85 us: per_device(): before = lax.ppermute(activations[:, rows - layers:], 'row', downward)]
    pallas_call x0 -> x4, Pallas kernels: none -> 78.9 us  [the longest x1 46.7 us: per_device(): call(across_kernel, jax.ShapeDtypeStruct((width, 2 * rows, DISPARITIES),...]
    reduce_min x548 -> x0, other arithmetic: 68.7 us -> none  [advance(): least = jnp.min(state, axis=-1, keepdims=True)]
    ppermute x32 -> x3, waiting for transfers between devices: 54.2 us -> 3.58 us  [the longest x1 3.58 us: per_device(): after = lax.ppermute(activations[:, :layers], 'row', upward)]
    all_gather x0 -> x2, waiting for transfers between devices: none -> 47 us  [the longest x1 27.1 us: per_device(): gathered = lax.all_gather(own, 'row', axis=0, axis_index_groups=groups)]
    slice x549 -> x1, local copies, waits for them, and re-layouts: 41.4 us -> 1.01 us  [per_device(): before = lax.ppermute(activations[:, rows - layers:], 'row', downward)]
    dynamic_update_slice x520 -> x0, other arithmetic: 40.3 us -> none  [the longest x512 39.6 us: sweep(): return lax.scan(stepper, incoming, costs, reverse=backward)]
    all_gather x1 -> x0, blocking collectives: 12.1 us -> none  [per_device(): lax.all_gather(right_normalized_features, 'col', axis=2, tiled=True)]
  transfers between devices with their start and end apart: 32 -> 5, of which waited for: 23 -> 3; matrix products, arithmetic and copies ran while one was open for 19% -> 2% of each run, Pallas kernels for 0% -> 29%
where the time goes in v1:
time: 160 us
  Pallas kernels  78.9 us (49%)
  waiting for transfers between devices  50.6 us (32%)
  between operations  14.2 us (9%)
  starting transfers between devices  8.59 us (5%)
  local copies, waits for them, and re-layouts  4.66 us (3%)
  other arithmetic  2.6 us (2%)
    pallas_call x1, Pallas kernels, per_device(): call(across_kernel, jax.ShapeDtypeStruct((width, 2 * rows, DISPARITIES),...  46.7 us
    all_gather x1, waiting for transfers between devices, per_device(): gathered = lax.all_gather(own, 'row', axis=0, axis_index_groups=groups)  27.1 us
    pallas_call x1, Pallas kernels, per_device(): call(band_kernel, (jax.ShapeDtypeStruct((cols, rows, DISPARITIES), f32),...  25.5 us
    all_gather x1, waiting for transfers between devices, per_device(): given = lax.all_gather(block, 'col', axis=0)  19.9 us
    ppermute x1, starting transfers between devices, per_device(): before = lax.ppermute(activations[:, rows - layers:], 'row', downward)  4.85 us
    pallas_call x1, Pallas kernels, per_device(): call(second_vertical_kernel, jax.ShapeDtypeStruct((rows, width, DISPARITI...  3.88 us
    ppermute x1, waiting for transfers between devices, per_device(): after = lax.ppermute(activations[:, :layers], 'row', upward)  3.58 us
  transfers between devices with their start and end apart: 5, of which 3 were waited for; matrix products, arithmetic and copies ran while one was open for 2% of the time, Pallas kernels for 29%

profile of v1, /device:TPU:0, one launch (start us, length us, event | category | flops | bytes accessed | tf_op | source)
XLA Modules:
  0.0 159.5 jit_solution(5112533998700025166)
XLA Ops:
  6.5 0.0 all-gather.5.cloned.1.call-start
  6.5 1.0 fusion
  7.5 4.8 %collective-permute-start = (bf16[2,3,64,128]{3,2,1,0:T(8,128)(2,1)S(1)}, bf16[2,3,64,128]{3,2,1,0:T(8,128)(2,1)S(1)}, u32[]{:S(2)}, u32[]{:S(2)}) collective-permute-start(bf16[2,3,64,128]{3,2,1,0:T(8,128)(2,1)S(1)} %get-tuple-element.13), channel_id=1, source_target_pairs={{0,4},{4,8},{8,12},{12,16},{16,20},{20,24},{24,28},{1,5},{5,9},{9,... | collective-permute-start | bytes 294920 | tf_op jit(solution)/shard_map/ppermute | solution.py:278
  12.4 1.3 collective-permute-start.1
  13.7 0.7 convert_element_type.6
  15.1 0.1 pad.4.clone
  15.1 0.1 pad.3.clone
  15.2 0.1 maximum_bitcast_fusion
  15.3 0.0 copy-start.1
  15.3 0.0 collective-permute-done
  15.3 3.6 %collective-permute-done.1 = bf16[2,3,64,128]{3,2,1,0:T(8,128)(2,1)S(1)} collective-permute-done((bf16[2,3,64,128]{3,2,1,0:T(8,128)(2,1)S(1)}, bf16[2,3,64,128]{3,2,1,0:T(8,128)(2,1)S(1)}, u32[]{:S(2)}, u32[]{:S(2)}) %collective-permute-start.1) | collective-permute-done | bytes 98336 | tf_op jit(solution)/shard_map/ppermute | solution.py:279
  18.9 1.0 pad_maximum_fusion.1
  19.9 0.8 pad_maximum_fusion
  20.7 0.0 all-gather.5.cloned.1.call-update
  20.8 0.0 all-gather.7.cloned.1.call-start
  20.8 0.0 copy-done
  20.8 0.4 copy.10
  21.2 1.1 reshape.7.filter_ref
  22.3 0.0 copy-done.1
  22.3 0.8 copy.11.bias_ref
  23.1 0.7 stack.19.place_ref
  23.7 19.9 %all-gather.5.cloned.1.call-done = bf16[116,64,128]{2,1,0:T(8,128)(2,1)} async-done(((bf16[29,64,128]{2,1,0:T(8,128)(2,1)}), bf16[116,64,128]{2,1,0:T(8,128)(2,1)}) %all-gather.5.cloned.1.call-update) | async-done | bytes 1900560 | tf_op jit(solution)/shard_map/all_gather | solution.py:290
  43.6 25.5 %shard_map.64 = (f32[512,8,128]{2,1,0:T(8,128)}, bf16[8,128,128]{2,1,0:T(8,128)(2,1)}) custom-call(s32[5]{0:T(128)} %stack.19.place_ref, bf16[4,29,64,128]{3,2,1,0:T(8,128)(2,1)} %bitcast.15, bf16[3,192,192]{2,1,0:T(8,128)(2,1)} %reshape.7.filter_ref, f32[3,64,1]{2,1,0:T(8,128)} %copy.11.bias_ref), custom_call_target="tpu_custom_call" | custom-call | flops 10000000000 | bytes 4194304 | tf_op jit(solution)/shard_map/pallas_call | solution.py:295
  69.2 0.0 all-gather.7.cloned.1.call-update
  69.2 27.1 %all-gather.7.cloned.1.call-done = bf16[32,128,128]{2,1,0:T(8,128)(2,1)} async-done(((bf16[8,128,128]{2,1,0:T(8,128)(2,1)}), bf16[32,128,128]{2,1,0:T(8,128)(2,1)}) %all-gather.7.cloned.1.call-update) | async-done | bytes 1048592 | tf_op jit(solution)/shard_map/all_gather | solution.py:313
  96.3 2.8 %shard_map.65 = (f32[8,128,128]{2,1,0:T(8,128)}, bf16[128,128]{1,0:T(8,128)(2,1)}) custom-call(s32[5]{0:T(128)} %stack.19.place_ref, s32[2]{0:T(128)} %charge_ref.5, bf16[4,8,128,128]{3,2,1,0:T(8,128)(2,1)} %bitcast.16), custom_call_target="tpu_custom_call" | custom-call | flops 2000000000 | bytes 4194304 | tf_op jit(solution)/shard_map/pallas_call | solution.py:322
  99.1 2.4 %collective-permute-start.2 = (bf16[128,128]{1,0:T(8,128)(2,1)}, bf16[128,128]{1,0:T(8,128)(2,1)S(1)}, u32[]{:S(2)}, u32[]{:S(2)}) collective-permute-start(bf16[128,128]{1,0:T(8,128)(2,1)} %get-tuple-element.11), channel_id=1, source_target_pairs={{0,16},{4,20},{8,24},{12,28},{16,0},{20,4},{24,8},{28,12},{1,17},{... | collective-permute-start | bytes 98312 | tf_op jit(solution)/shard_map/ppermute | solution.py:333
  101.5 46.7 %shard_map.66.across_ref = f32[128,16,128]{2,1,0:T(8,128)} custom-call(s32[5]{0:T(128)} %stack.19.place_ref, s32[2]{0:T(128)} %charge_ref.5, f32[512,8,128]{2,1,0:T(8,128)} %get-tuple-element.12.cost_ref), custom_call_target="tpu_custom_call" | custom-call | flops 20000000000 | bytes 4194304 | tf_op jit(solution)/shard_map/pallas_call | solution.py:315
  148.2 0.0 collective-permute-done.2.came_ref
  148.2 0.0 copy-start.2
  148.2 0.6 copy-done.2
  148.8 3.9 %shard_map.67 = f32[8,128,128]{2,1,0:T(8,128)} custom-call(s32[5]{0:T(128)} %stack.19.place_ref, s32[2]{0:T(128)} %charge_ref.5, bf16[4,8,128,128]{3,2,1,0:T(8,128)(2,1)} %bitcast.17, f32[8,128,128]{2,1,0:T(8,128)} %get-tuple-element.10.kept_ref, bf16[128,128]{1,0:T(8,128)(2,1)} %copy-done.2, f32[128,16,128]{2,1,0:T(8,128)} %shard_map.66.across_ref), custom_call_target="tpu_custom_call" | custom-call | flops 3000000000 | bytes 4194304 | tf_op jit(solution)/shard_map/pallas_call | solution.py:335
  (3 shorter events, 0.0 us)
Async XLA Ops:
  6.5 14.3 %copy-start = (bf16[3,3,3,64,64]{4,3,2,1,0:T(8,128)(2,1)S(1)}, bf16[3,3,3,64,64]{4,3,2,1,0:T(8,128)(2,1)}, u32[]{:S(2)}) copy-start(bf16[3,3,3,64,64]{4,3,2,1,0:T(8,128)(2,1)} %param.7) | copy-start | bytes 663556
  6.5 37.1 %all-gather.5.cloned.1.call-start = ((), (), s32[]{:S(2)}) async-start(), calls=%async_computation | async-start | bytes 2375680 | tf_op jit(solution)/shard_map/all_gather | solution.py:290
  7.5 7.8 %collective-permute-start = (bf16[2,3,64,128]{3,2,1,0:T(8,128)(2,1)S(1)}, bf16[2,3,64,128]{3,2,1,0:T(8,128)(2,1)S(1)}, u32[]{:S(2)}, u32[]{:S(2)}) collective-permute-start(bf16[2,3,64,128]{3,2,1,0:T(8,128)(2,1)S(1)} %get-tuple-element.13), channel_id=1, source_target_pairs={{0,4},{4,8},{8,12},{12,16},{16,20},{20,24},{24,28},{1,5},{5,9},{9,... | collective-permute-start | bytes 294920 | tf_op jit(solution)/shard_map/ppermute | solution.py:278
  12.4 6.5 %collective-permute-start.1 = (bf16[2,3,64,128]{3,2,1,0:T(8,128)(2,1)S(1)}, bf16[2,3,64,128]{3,2,1,0:T(8,128)(2,1)S(1)}, u32[]{:S(2)}, u32[]{:S(2)}) collective-permute-start(bf16[2,3,64,128]{3,2,1,0:T(8,128)(2,1)S(1)} %get-tuple-element.14), channel_id=1, source_target_pairs={{4,0},{8,4},{12,8},{16,12},{20,16},{24,20},{28,24},{5,1},{9,5},{13... | collective-permute-start | bytes 294920 | tf_op jit(solution)/shard_map/ppermute | solution.py:279
  15.3 7.0 %copy-start.1 = (f32[3,64]{1,0:T(4,128)S(1)}, f32[3,64]{1,0:T(4,128)}, u32[]{:S(2)}) copy-start(f32[3,64]{1,0:T(4,128)} %param.8) | copy-start | bytes 2308
  20.8 75.5 %all-gather.7.cloned.1.call-start = ((), (), s32[]{:S(2)}) async-start(), calls=%async_computation.1 | async-start | bytes 1310720 | tf_op jit(solution)/shard_map/all_gather | solution.py:313
  99.1 49.1 %collective-permute-start.2 = (bf16[128,128]{1,0:T(8,128)(2,1)}, bf16[128,128]{1,0:T(8,128)(2,1)S(1)}, u32[]{:S(2)}, u32[]{:S(2)}) collective-permute-start(bf16[128,128]{1,0:T(8,128)(2,1)} %get-tuple-element.11), channel_id=1, source_target_pairs={{0,16},{4,20},{8,24},{12,28},{16,0},{20,4},{24,8},{28,12},{1,17},{... | collective-permute-start | bytes 98312 | tf_op jit(solution)/shard_map/ppermute | solution.py:333
  148.2 0.6 copy-start.2
Sparse Core Ops, SparseCore 0:
  20.9 22.6 all-gather.4
  69.3 26.9 all-gather.6

commit v2 on v1

--- a/solution.py
+++ b/solution.py
@@ -121,7 +121,8 @@
         base = p * width - shift + lead
         block = base // width
         ahead = place + (base - block * width)
-        index = (ahead - lane_to_disparity(lane)) & (DISPARITIES - 1)
+        index = (ahead - lane) & (DISPARITIES - 1)
+        turned = (ahead - lane_to_disparity(lane)) & (DISPARITIES - 1)
         start = pl.multiple_of((block - 1) * width, width)
         here = pl.multiple_of(p * width, width)
         for y in range(rows):
@@ -132,12 +133,14 @@
             )
             chosen = jnp.where(lane <= ahead, product[:, width : 2 * width], product[:, :width])
             chosen = jnp.where(lane <= ahead - width, product[:, 2 * width :], chosen)
-            chosen = 1.0 - jnp.take_along_axis(chosen, index, axis=1, mode="promise_in_bounds")
-            cost_ref[pl.ds(here, width), y, :] = chosen
+            cost_ref[pl.ds(here, width), y, :] = 1.0 - jnp.take_along_axis(
+                chosen, index, axis=1, mode="promise_in_bounds"
+            )
 
             @pl.when(p == own)
             def _():
-                own_ref[y] = chosen.T.astype(jnp.bfloat16)
+                mine = jnp.take_along_axis(chosen, turned, axis=1, mode="promise_in_bounds")
+                own_ref[y] = (1.0 - mine).T.astype(jnp.bfloat16)
 
 
 def across_kernel(place_ref, charge_ref, cost_ref, kept_ref):
@@ -146,53 +149,52 @@
     parts = cols // width
     own = place_ref[2]
     p1, p2 = charges(charge_ref)
-
-    def step(i, state, keep, first_col, last_col):
-        right = cost_ref[first_col + i]
-        left = cost_ref[last_col - i]
-        cost = jnp.concatenate([right, left], axis=0).T
-        fresh = advance(list(state), registers(cost), p1, p2)
-        if keep:
-            back = jnp.concatenate(fresh, axis=0).T
-            kept_ref[i, 0:rows] = back[0:rows]
-            kept_ref[width - 1 - i, rows : 2 * rows] = back[rows : 2 * rows]
-        return tuple(fresh)
-
-    state = tuple(jnp.zeros((SUB, 2 * rows), jnp.float32) for _ in range(REGS))
-
-    def segment(p, state):
+    lane = lax.broadcasted_iota(jnp.int32, (rows, DISPARITIES), 1)
+    from_lower = jnp.where(lane == 0, jnp.inf, p1)
+    from_upper = jnp.where(lane == DISPARITIES - 1, jnp.inf, p1)
+
+    def one(state, jump, cost):
+        near = jnp.minimum(
+            pltpu.roll(state, 1, 1) + from_lower,
+            pltpu.roll(state, DISPARITIES - 1, 1) + from_upper,
+        )
+        walked = cost + jnp.minimum(state, near)
+        cheapest = jnp.min(cost, axis=1, keepdims=True)
+        fresh = jnp.minimum(walked, cost + jump)
+        least = jnp.minimum(jnp.min(walked, axis=1, keepdims=True), cheapest + jump)
+        return fresh, least + p2
+
+    def segment(p, carry):
         first_col = p * width
         last_col = cols - 1 - p * width
 
-        def plain(state):
-            return lax.fori_loop(
-                0, width, lambda i, s: step(i, s, False, first_col, last_col), state, unroll=8
-            )
-
-        def keeping(state):
-            def body(i, s):
-                right = cost_ref[first_col + i]
-                left = cost_ref[last_col - i]
-                cost = jnp.concatenate([right, left], axis=0).T
-                fresh = advance(list(s), registers(cost), p1, p2)
-                back = jnp.concatenate(fresh, axis=0).T
-
-                @pl.when(p == own)
-                def _():
-                    kept_ref[i, 0:rows] = back[0:rows]
-
-                @pl.when(parts - 1 - p == own)
-                def _():
-                    kept_ref[width - 1 - i, rows : 2 * rows] = back[rows : 2 * rows]
-
-                return tuple(fresh)
-
-            return lax.fori_loop(0, width, body, state, unroll=8)
-
-        mine = jnp.logical_or(p == own, parts - 1 - p == own)
-        return lax.cond(mine, keeping, plain, state)
-
-    lax.fori_loop(0, parts, segment, state)
+        def run(keep_right, keep_left, carry):
+            def body(i, carry):
+                right, right_jump, left, left_jump = carry
+                fresh_right, next_right = one(right, right_jump, cost_ref[first_col + i])
+                fresh_left, next_left = one(left, left_jump, cost_ref[last_col - i])
+                if keep_right:
+                    kept_ref[i, 0:rows] = fresh_right - (right_jump - p2)
+                if keep_left:
+                    kept_ref[width - 1 - i, rows : 2 * rows] = fresh_left - (left_jump - p2)
+                return fresh_right, next_right, fresh_left, next_left
+
+            return lax.fori_loop(0, width, body, carry, unroll=8)
+
+        choice = jnp.where(p == own, 1, 0) + jnp.where(parts - 1 - p == own, 2, 0)
+        carry = lax.switch(
+            choice,
+            [functools.partial(run, bool(k & 1), bool(k & 2)) for k in range(4)],
+            carry,
+        )
+        right, right_jump, left, left_jump = carry
+        right, left = right - (right_jump - p2), left - (left_jump - p2)
+        level = jnp.zeros_like(right_jump) + p2
+        return right, level, left, level
+
+    zero = jnp.zeros((rows, DISPARITIES), jnp.float32)
+    level = jnp.zeros((rows, 1), jnp.float32) + p2
+    lax.fori_loop(0, parts, segment, (zero, level, zero, level))
 
 
 def down_or_up(forward, first_own, cost_ref, state, p1, p2, keep):
@@ -215,9 +217,12 @@
     return lax.fori_loop(0, count, body, state, unroll=4)
 
 
-def first_vertical_kernel(place_ref, charge_ref, cost_ref, kept_ref, last_ref):
+def first_vertical_kernel(place_ref, charge_ref, *refs):
+    *block_refs, kept_ref, last_ref, cost_ref = refs
     p1, p2 = charges(charge_ref)
-    width = cost_ref.shape[-1]
+    group, _, _, width = cost_ref.shape
+    for k, block_ref in enumerate(block_refs):
+        cost_ref[lax.rem(place_ref[4] + group - k, group)] = block_ref[...]
     state = tuple(jnp.zeros((SUB, width), jnp.float32) for _ in range(REGS))
 
     def keep(row, value):
@@ -227,10 +232,12 @@
     last_ref[...] = jnp.concatenate(final, axis=0).astype(jnp.bfloat16)
 
 
-def second_vertical_kernel(
-    place_ref, charge_ref, cost_ref, kept_ref, came_ref, across_ref, out_ref, total
-):
+def second_vertical_kernel(place_ref, charge_ref, *refs):
+    *block_refs, kept_ref, came_ref, across_ref, out_ref, total, cost_ref = refs
     p1, p2 = charges(charge_ref)
+    group = cost_ref.shape[0]
+    for k, block_ref in enumerate(block_refs):
+        cost_ref[lax.rem(place_ref[4] + group - k, group)] = block_ref[...]
     rows, _, width = kept_ref.shape
     state = tuple(registers(came_ref[...].astype(jnp.float32)))
 
@@ -241,8 +248,8 @@
     lane = lax.broadcasted_iota(jnp.int32, (width, DISPARITIES), 1)
     index = disparity_to_lane(lane)
     for row in range(rows):
-        value = total[row].T + (across_ref[:, row, :] + across_ref[:, rows + row, :])
-        out_ref[row] = jnp.take_along_axis(value, index, axis=1, mode="promise_in_bounds")
+        vertical = jnp.take_along_axis(total[row].T, index, axis=1, mode="promise_in_bounds")
+        out_ref[row] = vertical + (across_ref[:, row, :] + across_ref[:, rows + row, :])
 
 
 SMEM = functools.partial(pl.BlockSpec, memory_space=pltpu.SMEM)
@@ -309,8 +316,10 @@
         flops=10**10,
     )(place, given, taps, biases[:, :, None])
 
-    groups = [list(range(half)), list(range(half, row_count))]
-    gathered = lax.all_gather(own, "row", axis=0, axis_index_groups=groups)
+    blocks = [own]
+    for k in range(1, half):
+        turn = [(i, i // half * half + (i + k) % half) for i in range(row_count)]
+        blocks.append(lax.ppermute(own, "row", turn))
 
     across = call(
         across_kernel,
@@ -318,16 +327,19 @@
         [SMEM(), SMEM(), VMEM()],
         flops=2 * 10**10,
     )(place, smooth, cost)
-
+    *blocks, across = lax.optimization_barrier((*blocks, across))
+
+    joined = pltpu.VMEM((half, rows, DISPARITIES, width), bf16)
     kept, last = call(
         first_vertical_kernel,
         (
             jax.ShapeDtypeStruct((rows, DISPARITIES, width), f32),
             jax.ShapeDtypeStruct((DISPARITIES, width), bf16),
         ),
-        [SMEM(), SMEM(), VMEM()],
+        [SMEM(), SMEM()] + [VMEM()] * half,
+        [joined],
         flops=2 * 10**9,
-    )(place, smooth, gathered)
+    )(place, smooth, *blocks)
 
     swap = [(i, (i + half) % row_count) for i in range(row_count)]
     came = lax.ppermute(last, "row", swap)
@@ -335,10 +347,10 @@
     return call(
         second_vertical_kernel,
         jax.ShapeDtypeStruct((rows, width, DISPARITIES), f32),
-        [SMEM(), SMEM(), VMEM(), VMEM(), VMEM(), VMEM()],
-        [pltpu.VMEM((rows, DISPARITIES, width), f32)],
+        [SMEM(), SMEM()] + [VMEM()] * (half + 3),
+        [pltpu.VMEM((rows, DISPARITIES, width), f32), joined],
         flops=3 * 10**9,
-    )(place, smooth, gathered, kept, came, across)
+    )(place, smooth, *blocks, kept, came, across)
 
 
 def solution(mesh):

time: 160 us -> 145 us (0.906)
  waiting for transfers between devices: 50.6 us -> 26.2 us
  Pallas kernels: 78.9 us -> 83.7 us
  starting transfers between devices: 8.59 us -> 12 us
    all_gather x1 -> x0, waiting for transfers between devices: 27.1 us -> none  [per_device(): gathered = lax.all_gather(own, 'row', axis=0, axis_index_groups=groups)]
    pallas_call x1, Pallas kernels: 46.7 us -> 50.5 us  [per_device(): call(across_kernel, jax.ShapeDtypeStruct((width, 2 * rows, DISPARITIES),...]
    ppermute x0 -> x3, starting transfers between devices: none -> 3.5 us  [per_device(): blocks.append(lax.ppermute(own, 'row', turn))]
    ppermute x1, waiting for transfers between devices: 0.01 us -> 2.64 us  [per_device(): came = lax.ppermute(last, 'row', swap)]
  transfers between devices with their start and end apart: 5 -> 7, of which waited for: 3 -> 3; matrix products, arithmetic and copies ran while one was open for 2% -> 3% of each run, Pallas kernels for 29% -> 35%
where the time goes in v2:
time: 145 us
  Pallas kernels  83.7 us (58%)
  waiting for transfers between devices  26.2 us (18%)
  between operations  14.2 us (10%)
  starting transfers between devices  12 us (8%)
  local copies, waits for them, and re-layouts  6.09 us (4%)
  other arithmetic  2.59 us (2%)
    pallas_call x1, Pallas kernels, per_device(): call(across_kernel, jax.ShapeDtypeStruct((width, 2 * rows, DISPARITIES),...  50.5 us
    pallas_call x1, Pallas kernels, per_device(): call(band_kernel, (jax.ShapeDtypeStruct((cols, rows, DISPARITIES), f32),...  26.5 us
    all_gather x1, waiting for transfers between devices, per_device(): given = lax.all_gather(block, 'col', axis=0)  20 us
    ppermute x1, starting transfers between devices, per_device(): before = lax.ppermute(activations[:, rows - layers:], 'row', downward)  4.85 us
    pallas_call x1, Pallas kernels, per_device(): call(second_vertical_kernel, jax.ShapeDtypeStruct((rows, width, DISPARITI...  3.97 us
    ppermute x1, waiting for transfers between devices, per_device(): after = lax.ppermute(activations[:, :layers], 'row', upward)  3.6 us
    ppermute x3, starting transfers between devices, per_device(): blocks.append(lax.ppermute(own, 'row', turn))  3.5 us
  transfers between devices with their start and end apart: 7, of which 3 were waited for; matrix products, arithmetic and copies ran while one was open for 3% of the time, Pallas kernels for 35%

profile of v2, /device:TPU:0, one launch (start us, length us, event | category | flops | bytes accessed | tf_op | source)
XLA Modules:
  0.0 144.9 jit_solution(8870712262356344927)
XLA Ops:
  6.5 1.0 fusion
  7.6 4.8 %collective-permute-start = (bf16[2,3,64,128]{3,2,1,0:T(8,128)(2,1)S(1)}, bf16[2,3,64,128]{3,2,1,0:T(8,128)(2,1)S(1)}, u32[]{:S(2)}, u32[]{:S(2)}) collective-permute-start(bf16[2,3,64,128]{3,2,1,0:T(8,128)(2,1)S(1)} %get-tuple-element.23), channel_id=1, source_target_pairs={{0,4},{4,8},{8,12},{12,16},{16,20},{20,24},{24,28},{1,5},{5,9},{9,... | collective-permute-start | bytes 294920 | tf_op jit(solution)/shard_map/ppermute | solution.py:285
  12.4 1.3 collective-permute-start.1
  14.4 0.1 pad.4.clone
  14.5 0.1 pad.3.clone
  14.5 0.7 convert_element_type.6
  15.2 0.1 maximum_bitcast_fusion
  15.3 0.0 collective-permute-done
  15.3 3.6 %collective-permute-done.1 = bf16[2,3,64,128]{3,2,1,0:T(8,128)(2,1)S(1)} collective-permute-done((bf16[2,3,64,128]{3,2,1,0:T(8,128)(2,1)S(1)}, bf16[2,3,64,128]{3,2,1,0:T(8,128)(2,1)S(1)}, u32[]{:S(2)}, u32[]{:S(2)}) %collective-permute-start.1) | collective-permute-done | bytes 98336 | tf_op jit(solution)/shard_map/ppermute | solution.py:286
  18.9 1.0 pad_maximum_fusion.1
  19.9 0.8 pad_maximum_fusion
  20.7 0.0 all-gather.3.cloned.1.call-update
  20.8 0.7 copy.11.bias_ref
  21.5 0.4 copy.10
  21.9 1.1 reshape.7.filter_ref
  23.0 0.6 stack.19.place_ref
  23.6 20.0 %all-gather.3.cloned.1.call-done = bf16[116,64,128]{2,1,0:T(8,128)(2,1)} async-done(((bf16[29,64,128]{2,1,0:T(8,128)(2,1)}), bf16[116,64,128]{2,1,0:T(8,128)(2,1)}) %all-gather.3.cloned.1.call-update) | async-done | bytes 1900560 | tf_op jit(solution)/shard_map/all_gather | solution.py:297
  43.6 26.5 %shard_map.64 = (f32[512,8,128]{2,1,0:T(8,128)}, bf16[8,128,128]{2,1,0:T(8,128)(2,1)}) custom-call(s32[5]{0:T(128)} %stack.19.place_ref, bf16[4,29,64,128]{3,2,1,0:T(8,128)(2,1)} %bitcast.14, bf16[3,192,192]{2,1,0:T(8,128)(2,1)} %reshape.7.filter_ref, f32[3,64,1]{2,1,0:T(8,128)} %copy.11.bias_ref), custom_call_target="tpu_custom_call" | custom-call | flops 10000000000 | bytes 4194304 | tf_op jit(solution)/shard_map/pallas_call | solution.py:302
  70.1 2.4 %collective-permute-start.4 = (bf16[8,128,128]{2,1,0:T(8,128)(2,1)}, bf16[8,128,128]{2,1,0:T(8,128)(2,1)S(1)}, u32[]{:S(2)}, u32[]{:S(2)}) collective-permute-start(bf16[8,128,128]{2,1,0:T(8,128)(2,1)} %get-tuple-element.16.refs_0_), channel_id=1, source_target_pairs={{0,12},{4,0},{8,4},{12,8},{16,28},{20,16},{24,20},{28,24},{1,13},{... | collective-permute-start | bytes 786440 | tf_op jit(solution)/shard_map/ppermute | solution.py:322
  72.5 0.5 collective-permute-start.3
  73.0 0.6 collective-permute-start.2
  73.6 50.5 %shard_map.65.refs_6_ = f32[128,16,128]{2,1,0:T(8,128)} custom-call(s32[5]{0:T(128)} %stack.19.place_ref, s32[2]{0:T(128)} %charge_ref.5, f32[512,8,128]{2,1,0:T(8,128)} %get-tuple-element.15.cost_ref), custom_call_target="tpu_custom_call" | custom-call | flops 20000000000 | bytes 4194304 | tf_op jit(solution)/shard_map/pallas_call | solution.py:324
  124.1 0.0 collective-permute-done.4.refs_3_
  124.1 0.0 collective-permute-done.3.refs_2_
  124.1 0.7 copy-done.2
  124.8 0.1 copy-done.3
  124.9 0.7 copy-done.4
  125.6 2.8 %shard_map.66 = (f32[8,128,128]{2,1,0:T(8,128)}, bf16[128,128]{1,0:T(8,128)(2,1)}) custom-call(s32[5]{0:T(128)} %stack.19.place_ref, s32[2]{0:T(128)} %charge_ref.5, bf16[8,128,128]{2,1,0:T(8,128)(2,1)} %get-tuple-element.16.refs_0_, bf16[8,128,128]{2,1,0:T(8,128)(2,1)} %copy-done.4, bf16[8,128,128]{2,1,0:T(8,128)(2,1)} %copy-done.3, ...), custom_call_target="tpu_custom_call" | custom-call | flops 2000000000 | bytes 4194304 | tf_op jit(solution)/shard_map/pallas_call | solution.py:333
  128.4 2.4 %collective-permute-start.5 = (bf16[128,128]{1,0:T(8,128)(2,1)}, bf16[128,128]{1,0:T(8,128)(2,1)S(1)}, u32[]{:S(2)}, u32[]{:S(2)}) collective-permute-start(bf16[128,128]{1,0:T(8,128)(2,1)} %get-tuple-element.21), channel_id=1, source_target_pairs={{0,16},{4,20},{8,24},{12,28},{16,0},{20,4},{24,8},{28,12},{1,17},{... | collective-permute-start | bytes 98312 | tf_op jit(solution)/shard_map/ppermute | solution.py:345
  130.8 2.6 %collective-permute-done.5.refs_5_ = bf16[128,128]{1,0:T(8,128)(2,1)S(1)} collective-permute-done((bf16[128,128]{1,0:T(8,128)(2,1)}, bf16[128,128]{1,0:T(8,128)(2,1)S(1)}, u32[]{:S(2)}, u32[]{:S(2)}) %collective-permute-start.5) | collective-permute-done | bytes 32800 | tf_op jit(solution)/shard_map/ppermute | solution.py:345
  133.4 0.6 copy-done.5
  134.1 4.0 %shard_map.67 = f32[8,128,128]{2,1,0:T(8,128)} custom-call(s32[5]{0:T(128)} %stack.19.place_ref, s32[2]{0:T(128)} %charge_ref.5, bf16[8,128,128]{2,1,0:T(8,128)(2,1)} %get-tuple-element.16.refs_0_, bf16[8,128,128]{2,1,0:T(8,128)(2,1)} %copy-done.4, bf16[8,128,128]{2,1,0:T(8,128)(2,1)} %copy-done.3, bf16[8,128,128]{2,1,0:T(8,128)(2,1)} %copy-done.2, ...), custom_call_target="tpu_custom_call" | custom-call | flops 3000000000 | bytes 4194304 | tf_op jit(solution)/shard_map/pallas_call | solution.py:347
  (12 shorter events, 0.0 us)
Async XLA Ops:
  6.5 14.3 %copy-start.1 = (f32[3,64]{1,0:T(4,128)S(1)}, f32[3,64]{1,0:T(4,128)}, u32[]{:S(2)}) copy-start(f32[3,64]{1,0:T(4,128)} %param.8) | copy-start | bytes 2308
  6.5 15.0 %copy-start = (bf16[3,3,3,64,64]{4,3,2,1,0:T(8,128)(2,1)S(1)}, bf16[3,3,3,64,64]{4,3,2,1,0:T(8,128)(2,1)}, u32[]{:S(2)}) copy-start(bf16[3,3,3,64,64]{4,3,2,1,0:T(8,128)(2,1)} %param.7) | copy-start | bytes 663556
  6.5 37.1 %all-gather.3.cloned.1.call-start = ((), (), s32[]{:S(2)}) async-start(), calls=%async_computation | async-start | bytes 2375680 | tf_op jit(solution)/shard_map/all_gather | solution.py:297
  7.6 7.8 %collective-permute-start = (bf16[2,3,64,128]{3,2,1,0:T(8,128)(2,1)S(1)}, bf16[2,3,64,128]{3,2,1,0:T(8,128)(2,1)S(1)}, u32[]{:S(2)}, u32[]{:S(2)}) collective-permute-start(bf16[2,3,64,128]{3,2,1,0:T(8,128)(2,1)S(1)} %get-tuple-element.23), channel_id=1, source_target_pairs={{0,4},{4,8},{8,12},{12,16},{16,20},{20,24},{24,28},{1,5},{5,9},{9,... | collective-permute-start | bytes 294920 | tf_op jit(solution)/shard_map/ppermute | solution.py:285
  12.4 6.5 %collective-permute-start.1 = (bf16[2,3,64,128]{3,2,1,0:T(8,128)(2,1)S(1)}, bf16[2,3,64,128]{3,2,1,0:T(8,128)(2,1)S(1)}, u32[]{:S(2)}, u32[]{:S(2)}) collective-permute-start(bf16[2,3,64,128]{3,2,1,0:T(8,128)(2,1)S(1)} %get-tuple-element.24), channel_id=1, source_target_pairs={{4,0},{8,4},{12,8},{16,12},{20,16},{24,20},{28,24},{5,1},{9,5},{13... | collective-permute-start | bytes 294920 | tf_op jit(solution)/shard_map/ppermute | solution.py:286
  70.1 54.0 %collective-permute-start.4 = (bf16[8,128,128]{2,1,0:T(8,128)(2,1)}, bf16[8,128,128]{2,1,0:T(8,128)(2,1)S(1)}, u32[]{:S(2)}, u32[]{:S(2)}) collective-permute-start(bf16[8,128,128]{2,1,0:T(8,128)(2,1)} %get-tuple-element.16.refs_0_), channel_id=1, source_target_pairs={{0,12},{4,0},{8,4},{12,8},{16,28},{20,16},{24,20},{28,24},{1,13},{... | collective-permute-start | bytes 786440 | tf_op jit(solution)/shard_map/ppermute | solution.py:322
  72.5 51.6 %collective-permute-start.3 = (bf16[8,128,128]{2,1,0:T(8,128)(2,1)}, bf16[8,128,128]{2,1,0:T(8,128)(2,1)S(1)}, u32[]{:S(2)}, u32[]{:S(2)}) collective-permute-start(bf16[8,128,128]{2,1,0:T(8,128)(2,1)} %get-tuple-element.16.refs_0_), channel_id=1, source_target_pairs={{0,8},{4,12},{8,0},{12,4},{16,24},{20,28},{24,16},{28,20},{1,9},{5... | collective-permute-start | bytes 786440 | tf_op jit(solution)/shard_map/ppermute | solution.py:322
  73.0 51.1 %collective-permute-start.2 = (bf16[8,128,128]{2,1,0:T(8,128)(2,1)}, bf16[8,128,128]{2,1,0:T(8,128)(2,1)S(1)}, u32[]{:S(2)}, u32[]{:S(2)}) collective-permute-start(bf16[8,128,128]{2,1,0:T(8,128)(2,1)} %get-tuple-element.16.refs_0_), channel_id=1, source_target_pairs={{0,4},{4,8},{8,12},{12,0},{16,20},{20,24},{24,28},{28,16},{1,5},{5... | collective-permute-start | bytes 786440 | tf_op jit(solution)/shard_map/ppermute | solution.py:322
  124.1 0.7 copy-start.2
  124.1 0.8 copy-start.3
  124.9 0.7 copy-start.4
  128.4 5.0 %collective-permute-start.5 = (bf16[128,128]{1,0:T(8,128)(2,1)}, bf16[128,128]{1,0:T(8,128)(2,1)S(1)}, u32[]{:S(2)}, u32[]{:S(2)}) collective-permute-start(bf16[128,128]{1,0:T(8,128)(2,1)} %get-tuple-element.21), channel_id=1, source_target_pairs={{0,16},{4,20},{8,24},{12,28},{16,0},{20,4},{24,8},{28,12},{1,17},{... | collective-permute-start | bytes 98312 | tf_op jit(solution)/shard_map/ppermute | solution.py:345
  133.4 0.6 copy-start.5
Sparse Core Ops, SparseCore 0:
  20.9 22.6 all-gather.2

commit v3 on v2

--- a/solution.py
+++ b/solution.py
@@ -31,8 +31,10 @@
     while len(least) > 1:
         least = [jnp.minimum(a, b) for a, b in zip(least[::2], least[1::2])]
     least = least[0]
-    for turn in (4, 2, 1):
-        least = jnp.minimum(least, pltpu.roll(least, turn, 0))
+    turned = [least] + [pltpu.roll(least, turn, 0) for turn in range(1, SUB)]
+    while len(turned) > 1:
+        turned = [jnp.minimum(a, b) for a, b in zip(turned[::2], turned[1::2])]
+    least = turned[0]
     lower = [below] + state[:-1]
     upper = state[1:] + [above]
     fresh = []
@@ -121,8 +123,7 @@
         base = p * width - shift + lead
         block = base // width
         ahead = place + (base - block * width)
-        index = (ahead - lane) & (DISPARITIES - 1)
-        turned = (ahead - lane_to_disparity(lane)) & (DISPARITIES - 1)
+        index = (ahead - lane_to_disparity(lane)) & (DISPARITIES - 1)
         start = pl.multiple_of((block - 1) * width, width)
         here = pl.multiple_of(p * width, width)
         for y in range(rows):
@@ -133,14 +134,12 @@
             )
             chosen = jnp.where(lane <= ahead, product[:, width : 2 * width], product[:, :width])
             chosen = jnp.where(lane <= ahead - width, product[:, 2 * width :], chosen)
-            cost_ref[pl.ds(here, width), y, :] = 1.0 - jnp.take_along_axis(
-                chosen, index, axis=1, mode="promise_in_bounds"
-            )
+            chosen = 1.0 - jnp.take_along_axis(chosen, index, axis=1, mode="promise_in_bounds")
+            cost_ref[pl.ds(here, width), y, :] = chosen
 
             @pl.when(p == own)
             def _():
-                mine = jnp.take_along_axis(chosen, turned, axis=1, mode="promise_in_bounds")
-                own_ref[y] = (1.0 - mine).T.astype(jnp.bfloat16)
+                own_ref[y] = chosen.T.astype(jnp.bfloat16)
 
 
 def across_kernel(place_ref, charge_ref, cost_ref, kept_ref):
@@ -149,72 +148,60 @@
     parts = cols // width
     own = place_ref[2]
     p1, p2 = charges(charge_ref)
-    lane = lax.broadcasted_iota(jnp.int32, (rows, DISPARITIES), 1)
-    from_lower = jnp.where(lane == 0, jnp.inf, p1)
-    from_upper = jnp.where(lane == DISPARITIES - 1, jnp.inf, p1)
-
-    def one(state, jump, cost):
-        near = jnp.minimum(
-            pltpu.roll(state, 1, 1) + from_lower,
-            pltpu.roll(state, DISPARITIES - 1, 1) + from_upper,
-        )
-        walked = cost + jnp.minimum(state, near)
-        cheapest = jnp.min(cost, axis=1, keepdims=True)
-        fresh = jnp.minimum(walked, cost + jump)
-        least = jnp.minimum(jnp.min(walked, axis=1, keepdims=True), cheapest + jump)
-        return fresh, least + p2
-
-    def segment(p, carry):
+
+    def segment(p, state):
         first_col = p * width
         last_col = cols - 1 - p * width
 
-        def run(keep_right, keep_left, carry):
-            def body(i, carry):
-                right, right_jump, left, left_jump = carry
-                fresh_right, next_right = one(right, right_jump, cost_ref[first_col + i])
-                fresh_left, next_left = one(left, left_jump, cost_ref[last_col - i])
+        def run(keep_right, keep_left, state):
+            def body(i, state):
+                pair = [cost_ref[first_col + i], cost_ref[last_col - i]]
+                cost = jnp.concatenate(pair, axis=0).T
+                fresh = advance(list(state), registers(cost), p1, p2)
+                if keep_right or keep_left:
+                    back = jnp.concatenate(fresh, axis=0).T
                 if keep_right:
-                    kept_ref[i, 0:rows] = fresh_right - (right_jump - p2)
+                    kept_ref[i, 0:rows] = back[0:rows]
                 if keep_left:
-                    kept_ref[width - 1 - i, rows : 2 * rows] = fresh_left - (left_jump - p2)
-                return fresh_right, next_right, fresh_left, next_left
-
-            return lax.fori_loop(0, width, body, carry, unroll=8)
+                    kept_ref[width - 1 - i, rows : 2 * rows] = back[rows : 2 * rows]
+                return tuple(fresh)
+
+            return lax.fori_loop(0, width, body, state, unroll=8)
 
         choice = jnp.where(p == own, 1, 0) + jnp.where(parts - 1 - p == own, 2, 0)
-        carry = lax.switch(
+        return lax.switch(
             choice,
             [functools.partial(run, bool(k & 1), bool(k & 2)) for k in range(4)],
-            carry,
+            state,
         )
-        right, right_jump, left, left_jump = carry
-        right, left = right - (right_jump - p2), left - (left_jump - p2)
-        level = jnp.zeros_like(right_jump) + p2
-        return right, level, left, level
-
-    zero = jnp.zeros((rows, DISPARITIES), jnp.float32)
-    level = jnp.zeros((rows, 1), jnp.float32) + p2
-    lax.fori_loop(0, parts, segment, (zero, level, zero, level))
+
+    state = tuple(jnp.zeros((SUB, 2 * rows), jnp.float32) for _ in range(REGS))
+    lax.fori_loop(0, parts, segment, state)
 
 
 def down_or_up(forward, first_own, cost_ref, state, p1, p2, keep):
     group, rows = cost_ref.shape[:2]
-    count = group * rows
-
-    def body(i, state):
-        row = jnp.where(forward, i, count - 1 - i)
-        block = row // rows
-        inner = row - block * rows
-        cost = cost_ref[block, inner].astype(jnp.float32)
-        fresh = advance(list(state), registers(cost), p1, p2)
-
-        @pl.when(block == first_own)
-        def _():
-            keep(inner, jnp.concatenate(fresh, axis=0))
-
-        return tuple(fresh)
-
-    return lax.fori_loop(0, count, body, state, unroll=4)
+
+    def block(b, state):
+        member = jnp.where(forward, b, group - 1 - b)
+
+        def run(kept, state):
+            for i in range(rows):
+                inner = jnp.where(forward, i, rows - 1 - i)
+                cost = cost_ref[member, inner].astype(jnp.float32)
+                state = advance(list(state), registers(cost), p1, p2)
+                if kept:
+                    keep(inner, jnp.concatenate(state, axis=0))
+            return tuple(state)
+
+        return lax.cond(
+            member == first_own,
+            functools.partial(run, True),
+            functools.partial(run, False),
+            state,
+        )
+
+    return lax.fori_loop(0, group, block, state)
 
 
 def first_vertical_kernel(place_ref, charge_ref, *refs):
@@ -248,8 +235,8 @@
     lane = lax.broadcasted_iota(jnp.int32, (width, DISPARITIES), 1)
     index = disparity_to_lane(lane)
     for row in range(rows):
-        vertical = jnp.take_along_axis(total[row].T, index, axis=1, mode="promise_in_bounds")
-        out_ref[row] = vertical + (across_ref[:, row, :] + across_ref[:, rows + row, :])
+        value = total[row].T + (across_ref[:, row, :] + across_ref[:, rows + row, :])
+        out_ref[row] = jnp.take_along_axis(value, index, axis=1, mode="promise_in_bounds")
 
 
 SMEM = functools.partial(pl.BlockSpec, memory_space=pltpu.SMEM)

time: 145 us -> 120 us (0.83)
  Pallas kernels: 83.7 us -> 58 us
    pallas_call x1, Pallas kernels: 50.5 us -> 25.8 us  [per_device(): call(across_kernel, jax.ShapeDtypeStruct((width, 2 * rows, DISPARITIES),...]
  transfers between devices with their start and end apart: 7 -> 7, of which waited for: 3 -> 3; matrix products, arithmetic and copies ran while one was open for 3% -> 3% of each run, Pallas kernels for 35% -> 22%
where the time goes in v3:
time: 120 us; the launch traced here: 119 us
  Pallas kernels  58 us (48%)
  waiting for transfers between devices  26.2 us (22%)
  between operations  14.1 us (12%)
  starting transfers between devices  12 us (10%)
  local copies, waits for them, and re-layouts  6.09 us (5%)
  other arithmetic  2.59 us (2%)
    pallas_call x1, Pallas kernels, per_device(): call(across_kernel, jax.ShapeDtypeStruct((width, 2 * rows, DISPARITIES),...  25.8 us
    pallas_call x1, Pallas kernels, per_device(): call(band_kernel, (jax.ShapeDtypeStruct((cols, rows, DISPARITIES), f32),...  25.6 us
    all_gather x1, waiting for transfers between devices, per_device(): given = lax.all_gather(block, 'col', axis=0)  20 us
    ppermute x1, starting transfers between devices, per_device(): before = lax.ppermute(activations[:, rows - layers:], 'row', downward)  4.85 us
    pallas_call x1, Pallas kernels, per_device(): call(second_vertical_kernel, jax.ShapeDtypeStruct((rows, width, DISPARITI...  3.9 us
    ppermute x1, waiting for transfers between devices, per_device(): after = lax.ppermute(activations[:, :layers], 'row', upward)  3.6 us
    ppermute x3, starting transfers between devices, per_device(): blocks.append(lax.ppermute(own, 'row', turn))  3.49 us
    pallas_call x1, Pallas kernels, per_device(): call(first_vertical_kernel, (jax.ShapeDtypeStruct((rows, DISPARITIES, wid...  2.74 us
  transfers between devices with their start and end apart: 7, of which 3 were waited for; matrix products, arithmetic and copies ran while one was open for 3% of the time, Pallas kernels for 22%

profile of v3, /device:TPU:0, one launch (start us, length us, event | category | flops | bytes accessed | tf_op | source)
XLA Modules:
  0.0 119.1 jit_solution(11898863862143810340)
XLA Ops:
  6.5 1.0 fusion
  7.6 4.8 %collective-permute-start = (bf16[2,3,64,128]{3,2,1,0:T(8,128)(2,1)S(1)}, bf16[2,3,64,128]{3,2,1,0:T(8,128)(2,1)S(1)}, u32[]{:S(2)}, u32[]{:S(2)}) collective-permute-start(bf16[2,3,64,128]{3,2,1,0:T(8,128)(2,1)S(1)} %get-tuple-element.23), channel_id=1, source_target_pairs={{0,4},{4,8},{8,12},{12,16},{16,20},{20,24},{24,28},{1,5},{5,9},{9,... | collective-permute-start | bytes 294920 | tf_op jit(solution)/shard_map/ppermute | solution.py:272
  12.4 1.3 %collective-permute-start.1 = (bf16[2,3,64,128]{3,2,1,0:T(8,128)(2,1)S(1)}, bf16[2,3,64,128]{3,2,1,0:T(8,128)(2,1)S(1)}, u32[]{:S(2)}, u32[]{:S(2)}) collective-permute-start(bf16[2,3,64,128]{3,2,1,0:T(8,128)(2,1)S(1)} %get-tuple-element.24), channel_id=1, source_target_pairs={{4,0},{8,4},{12,8},{16,12},{20,16},{24,20},{28,24},{5,1},{9,5},{13... | collective-permute-start | bytes 294920 | tf_op jit(solution)/shard_map/ppermute | solution.py:273
  14.4 0.1 pad.4.clone
  14.5 0.1 pad.3.clone
  14.5 0.7 convert_element_type.6
  15.2 0.1 maximum_bitcast_fusion
  15.3 0.0 collective-permute-done
  15.3 3.6 %collective-permute-done.1 = bf16[2,3,64,128]{3,2,1,0:T(8,128)(2,1)S(1)} collective-permute-done((bf16[2,3,64,128]{3,2,1,0:T(8,128)(2,1)S(1)}, bf16[2,3,64,128]{3,2,1,0:T(8,128)(2,1)S(1)}, u32[]{:S(2)}, u32[]{:S(2)}) %collective-permute-start.1) | collective-permute-done | bytes 98336 | tf_op jit(solution)/shard_map/ppermute | solution.py:273
  18.9 1.0 pad_maximum_fusion.1
  19.9 0.8 pad_maximum_fusion
  20.7 0.0 all-gather.3.cloned.1.call-update
  20.8 0.7 copy.11.bias_ref
  21.5 0.4 copy.10
  21.9 1.1 reshape.7.filter_ref
  23.0 0.6 stack.19.place_ref
  23.6 20.0 %all-gather.3.cloned.1.call-done = bf16[116,64,128]{2,1,0:T(8,128)(2,1)} async-done(((bf16[29,64,128]{2,1,0:T(8,128)(2,1)}), bf16[116,64,128]{2,1,0:T(8,128)(2,1)}) %all-gather.3.cloned.1.call-update) | async-done | bytes 1900560 | tf_op jit(solution)/shard_map/all_gather | solution.py:284
  43.6 25.6 %shard_map.64 = (f32[512,8,128]{2,1,0:T(8,128)}, bf16[8,128,128]{2,1,0:T(8,128)(2,1)}) custom-call(s32[5]{0:T(128)} %stack.19.place_ref, bf16[4,29,64,128]{3,2,1,0:T(8,128)(2,1)} %bitcast.14, bf16[3,192,192]{2,1,0:T(8,128)(2,1)} %reshape.7.filter_ref, f32[3,64,1]{2,1,0:T(8,128)} %copy.11.bias_ref), custom_call_target="tpu_custom_call" | custom-call | flops 10000000000 | bytes 4194304 | tf_op jit(solution)/shard_map/pallas_call | solution.py:289
  69.2 2.4 %collective-permute-start.4 = (bf16[8,128,128]{2,1,0:T(8,128)(2,1)}, bf16[8,128,128]{2,1,0:T(8,128)(2,1)S(1)}, u32[]{:S(2)}, u32[]{:S(2)}) collective-permute-start(bf16[8,128,128]{2,1,0:T(8,128)(2,1)} %get-tuple-element.16.refs_0_), channel_id=1, source_target_pairs={{0,12},{4,0},{8,4},{12,8},{16,28},{20,16},{24,20},{28,24},{1,13},{... | collective-permute-start | bytes 786440 | tf_op jit(solution)/shard_map/ppermute | solution.py:309
  71.6 0.5 collective-permute-start.3
  72.1 0.6 collective-permute-start.2
  72.7 25.8 %shard_map.65.refs_6_ = f32[128,16,128]{2,1,0:T(8,128)} custom-call(s32[5]{0:T(128)} %stack.19.place_ref, s32[2]{0:T(128)} %charge_ref.5, f32[512,8,128]{2,1,0:T(8,128)} %get-tuple-element.15.cost_ref), custom_call_target="tpu_custom_call" | custom-call | flops 20000000000 | bytes 4194304 | tf_op jit(solution)/shard_map/pallas_call | solution.py:311
  98.5 0.0 collective-permute-done.4.refs_3_
  98.5 0.0 collective-permute-done.2.refs_1_
  98.5 0.7 copy-done.2
  99.2 0.1 copy-done.3
  99.3 0.7 copy-done.4
  100.0 2.7 %shard_map.66 = (f32[8,128,128]{2,1,0:T(8,128)}, bf16[128,128]{1,0:T(8,128)(2,1)}) custom-call(s32[5]{0:T(128)} %stack.19.place_ref, s32[2]{0:T(128)} %charge_ref.5, bf16[8,128,128]{2,1,0:T(8,128)(2,1)} %get-tuple-element.16.refs_0_, bf16[8,128,128]{2,1,0:T(8,128)(2,1)} %copy-done.4, bf16[8,128,128]{2,1,0:T(8,128)(2,1)} %copy-done.3, ...), custom_call_target="tpu_custom_call" | custom-call | flops 2000000000 | bytes 4194304 | tf_op jit(solution)/shard_map/pallas_call | solution.py:320
  102.7 2.4 %collective-permute-start.5 = (bf16[128,128]{1,0:T(8,128)(2,1)}, bf16[128,128]{1,0:T(8,128)(2,1)S(1)}, u32[]{:S(2)}, u32[]{:S(2)}) collective-permute-start(bf16[128,128]{1,0:T(8,128)(2,1)} %get-tuple-element.21), channel_id=1, source_target_pairs={{0,16},{4,20},{8,24},{12,28},{16,0},{20,4},{24,8},{28,12},{1,17},{... | collective-permute-start | bytes 98312 | tf_op jit(solution)/shard_map/ppermute | solution.py:332
  105.2 2.6 %collective-permute-done.5.refs_5_ = bf16[128,128]{1,0:T(8,128)(2,1)S(1)} collective-permute-done((bf16[128,128]{1,0:T(8,128)(2,1)}, bf16[128,128]{1,0:T(8,128)(2,1)S(1)}, u32[]{:S(2)}, u32[]{:S(2)}) %collective-permute-start.5) | collective-permute-done | bytes 32800 | tf_op jit(solution)/shard_map/ppermute | solution.py:332
  107.8 0.6 copy-done.5
  108.4 3.9 %shard_map.67 = f32[8,128,128]{2,1,0:T(8,128)} custom-call(s32[5]{0:T(128)} %stack.19.place_ref, s32[2]{0:T(128)} %charge_ref.5, bf16[8,128,128]{2,1,0:T(8,128)(2,1)} %get-tuple-element.16.refs_0_, bf16[8,128,128]{2,1,0:T(8,128)(2,1)} %copy-done.4, bf16[8,128,128]{2,1,0:T(8,128)(2,1)} %copy-done.3, bf16[8,128,128]{2,1,0:T(8,128)(2,1)} %copy-done.2, ...), custom_call_target="tpu_custom_call" | custom-call | flops 3000000000 | bytes 4194304 | tf_op jit(solution)/shard_map/pallas_call | solution.py:334
  (12 shorter events, 0.0 us)
Async XLA Ops:
  6.5 14.3 %copy-start.1 = (f32[3,64]{1,0:T(4,128)S(1)}, f32[3,64]{1,0:T(4,128)}, u32[]{:S(2)}) copy-start(f32[3,64]{1,0:T(4,128)} %param.8) | copy-start | bytes 2308
  6.5 15.0 %copy-start = (bf16[3,3,3,64,64]{4,3,2,1,0:T(8,128)(2,1)S(1)}, bf16[3,3,3,64,64]{4,3,2,1,0:T(8,128)(2,1)}, u32[]{:S(2)}) copy-start(bf16[3,3,3,64,64]{4,3,2,1,0:T(8,128)(2,1)} %param.7) | copy-start | bytes 663556
  6.5 37.1 %all-gather.3.cloned.1.call-start = ((), (), s32[]{:S(2)}) async-start(), calls=%async_computation | async-start | bytes 2375680 | tf_op jit(solution)/shard_map/all_gather | solution.py:284
  7.6 7.8 %collective-permute-start = (bf16[2,3,64,128]{3,2,1,0:T(8,128)(2,1)S(1)}, bf16[2,3,64,128]{3,2,1,0:T(8,128)(2,1)S(1)}, u32[]{:S(2)}, u32[]{:S(2)}) collective-permute-start(bf16[2,3,64,128]{3,2,1,0:T(8,128)(2,1)S(1)} %get-tuple-element.23), channel_id=1, source_target_pairs={{0,4},{4,8},{8,12},{12,16},{16,20},{20,24},{24,28},{1,5},{5,9},{9,... | collective-permute-start | bytes 294920 | tf_op jit(solution)/shard_map/ppermute | solution.py:272
  12.4 6.5 %collective-permute-start.1 = (bf16[2,3,64,128]{3,2,1,0:T(8,128)(2,1)S(1)}, bf16[2,3,64,128]{3,2,1,0:T(8,128)(2,1)S(1)}, u32[]{:S(2)}, u32[]{:S(2)}) collective-permute-start(bf16[2,3,64,128]{3,2,1,0:T(8,128)(2,1)S(1)} %get-tuple-element.24), channel_id=1, source_target_pairs={{4,0},{8,4},{12,8},{16,12},{20,16},{24,20},{28,24},{5,1},{9,5},{13... | collective-permute-start | bytes 294920 | tf_op jit(solution)/shard_map/ppermute | solution.py:273
  69.2 29.3 %collective-permute-start.4 = (bf16[8,128,128]{2,1,0:T(8,128)(2,1)}, bf16[8,128,128]{2,1,0:T(8,128)(2,1)S(1)}, u32[]{:S(2)}, u32[]{:S(2)}) collective-permute-start(bf16[8,128,128]{2,1,0:T(8,128)(2,1)} %get-tuple-element.16.refs_0_), channel_id=1, source_target_pairs={{0,12},{4,0},{8,4},{12,8},{16,28},{20,16},{24,20},{28,24},{1,13},{... | collective-permute-start | bytes 786440 | tf_op jit(solution)/shard_map/ppermute | solution.py:309
  71.6 26.9 %collective-permute-start.3 = (bf16[8,128,128]{2,1,0:T(8,128)(2,1)}, bf16[8,128,128]{2,1,0:T(8,128)(2,1)S(1)}, u32[]{:S(2)}, u32[]{:S(2)}) collective-permute-start(bf16[8,128,128]{2,1,0:T(8,128)(2,1)} %get-tuple-element.16.refs_0_), channel_id=1, source_target_pairs={{0,8},{4,12},{8,0},{12,4},{16,24},{20,28},{24,16},{28,20},{1,9},{5... | collective-permute-start | bytes 786440 | tf_op jit(solution)/shard_map/ppermute | solution.py:309
  72.1 26.4 %collective-permute-start.2 = (bf16[8,128,128]{2,1,0:T(8,128)(2,1)}, bf16[8,128,128]{2,1,0:T(8,128)(2,1)S(1)}, u32[]{:S(2)}, u32[]{:S(2)}) collective-permute-start(bf16[8,128,128]{2,1,0:T(8,128)(2,1)} %get-tuple-element.16.refs_0_), channel_id=1, source_target_pairs={{0,4},{4,8},{8,12},{12,0},{16,20},{20,24},{24,28},{28,16},{1,5},{5... | collective-permute-start | bytes 786440 | tf_op jit(solution)/shard_map/ppermute | solution.py:309
  98.5 0.7 copy-start.2
  98.5 0.8 copy-start.3
  99.3 0.7 copy-start.4
  102.7 5.0 %collective-permute-start.5 = (bf16[128,128]{1,0:T(8,128)(2,1)}, bf16[128,128]{1,0:T(8,128)(2,1)S(1)}, u32[]{:S(2)}, u32[]{:S(2)}) collective-permute-start(bf16[128,128]{1,0:T(8,128)(2,1)} %get-tuple-element.21), channel_id=1, source_target_pairs={{0,16},{4,20},{8,24},{12,28},{16,0},{20,4},{24,8},{28,12},{1,17},{... | collective-permute-start | bytes 98312 | tf_op jit(solution)/shard_map/ppermute | solution.py:332
  107.8 0.6 copy-start.5
Sparse Core Ops, SparseCore 0:
  20.9 22.6 all-gather.2
